TPU v7x, 32 devices: a whole 2x2x4 slice. The times are simulated.
32 devices in a mesh: fsdp: 16 (over z, x, core), tp: 2 (over y).
Axes of the slice: x: 2, y: 2, z: 4, core: 2. Of those that a mesh axis runs over, the one named last changes fastest.
Arguments:
- inputs: bfloat16 [32, 736, 1152], P('fsdp', 'tp'), may hold values from -6 to 6
- w_qkv: bfloat16 [3, 1152, 1152], P(None, 'fsdp', 'tp'), may hold values from -0.25 to 0.25
- w_out: bfloat16 [1152, 1152], P('tp', 'fsdp'), may hold values from -0.75 to 0.75
- w_up: bfloat16 [1152, 4304], P('fsdp', 'tp'), may hold values from -0.1875 to 0.1875
- w_down: bfloat16 [4304, 1152], P('tp', 'fsdp'), may hold values from -0.09375 to 0.09375
- norm_gains: float32 [2, 1152], replicated, may hold values from 0.1 to 1.9
- biases: float32 [6, 1152], replicated, may hold values from -3 to 3
- up_bias: float32 [4304], replicated, may hold values from -3 to 3
- cotangent: bfloat16 [32, 736, 1152], P('fsdp', 'tp'), may hold values from -6 to 6
Outputs:
- outputs: bfloat16 [32, 736, 1152], P('fsdp', 'tp')
- input_grad: float32 [32, 736, 1152], P('fsdp', 'tp')
- w_qkv_grad: float32 [3, 1152, 1152], P(None, 'fsdp', 'tp')
- w_out_grad: float32 [1152, 1152], P('tp', 'fsdp')
- w_up_grad: float32 [1152, 4304], P('fsdp', 'tp')
- w_down_grad: float32 [4304, 1152], P('tp', 'fsdp')
- norm_gains_grad: float32 [2, 1152], replicated
- biases_grad: float32 [6, 1152], replicated
- up_bias_grad: float32 [4304], replicated
All inputs are finite; a program needn't handle non-finite values.
Results may differ from a plain program's by a relative error of at most 0.018.
The roundings to bfloat16 on the way count: a program that leaves them out, or rounds other values in their place, can miss the bound.
Values may be sent and summed in bfloat16 or wider, within the bound.
A program may use at most 192 MiB of HBM per device.

v0:
```python
import math

import jax
import jax.numpy as jnp
from jax import lax
from jax.sharding import PartitionSpec as P

HD = 72
VALID = 729


norm_eps = 1e-06
gelu_coef = math.sqrt(2.0 / math.pi)


def norm_forward(values, scale_row, shift_row):
    average = jnp.mean(values, axis=-1, keepdims=True)
    centred = values - average
    inv_std = lax.rsqrt(jnp.mean(centred * centred, axis=-1, keepdims=True) + norm_eps)
    normed = centred * inv_std
    return (normed * scale_row + shift_row, normed, inv_std)


def norm_backward(upstream, normed, inv_std, scale_row):
    scaled = upstream * scale_row
    back = inv_std * (
        scaled
        - jnp.mean(scaled, axis=-1, keepdims=True)
        - normed * jnp.mean(scaled * normed, axis=-1, keepdims=True)
    )
    return (back, jnp.sum(upstream * normed, axis=(0, 1)), jnp.sum(upstream, axis=(0, 1)))


def gelu_tanh(pre_act):
    return (
        0.5
        * pre_act
        * (1.0 + jnp.tanh(gelu_coef * (pre_act + 0.044715 * pre_act * pre_act * pre_act)))
    )


def gelu_slope(pre_act):
    tangent = jnp.tanh(gelu_coef * (pre_act + 0.044715 * pre_act * pre_act * pre_act))
    inner_slope = gelu_coef * (1.0 + 3.0 * 0.044715 * pre_act * pre_act)
    return 0.5 * (1.0 + tangent) + 0.5 * pre_act * (1.0 - tangent * tangent) * inner_slope


def masked_scores(queries, key_rows):
    seq_len = queries.shape[0]
    head_count = queries.shape[1] // HD
    query_heads = queries.reshape(seq_len, head_count, HD)
    key_heads = key_rows.reshape(seq_len, head_count, HD)
    scores = jnp.einsum("qhe,khe->hqk", query_heads, key_heads, preferred_element_type=jnp.float32)
    scores = scores * (1.0 / math.sqrt(HD))
    visible = lax.broadcasted_iota(jnp.int32, (1, 1, seq_len), 2) < VALID
    return (jnp.where(visible, scores, -1e30), query_heads, key_heads)


def attend_forward(triple):
    queries, key_rows, values = triple
    seq_len = queries.shape[0]
    scores, query_heads, key_heads = masked_scores(queries, key_rows)
    value_heads = values.reshape(seq_len, -1, HD)
    largest = jnp.max(scores, axis=-1, keepdims=True)
    powers = jnp.exp(scores - largest)
    summed = jnp.sum(powers, axis=-1, keepdims=True)
    attn_probs = (powers / summed).astype(jnp.bfloat16)
    mixed_out = jnp.einsum(
        "hqk,khe->qhe", attn_probs, value_heads, preferred_element_type=jnp.float32
    )
    log_totals = (largest + jnp.log(summed))[:, :, 0]
    return (mixed_out.reshape(seq_len, queries.shape[1]).astype(jnp.bfloat16), log_totals)


def attend_backward(items):
    queries, key_rows, values, log_totals, d_mixed = items
    seq_len = queries.shape[0]
    scores, query_heads, key_heads = masked_scores(queries, key_rows)
    value_heads = values.reshape(seq_len, -1, HD)
    grad_heads = d_mixed.reshape(seq_len, -1, HD)
    probs_full = jnp.exp(scores - log_totals[:, :, None])
    d_probs = jnp.einsum(
        "qhe,khe->hqk", grad_heads, value_heads, preferred_element_type=jnp.float32
    )
    row_inner = jnp.sum(probs_full * d_probs, axis=-1, keepdims=True)
    d_scores = (probs_full * (d_probs - row_inner)).astype(jnp.bfloat16)
    d_values = jnp.einsum(
        "hqk,qhe->khe",
        probs_full.astype(jnp.bfloat16),
        grad_heads,
        preferred_element_type=jnp.float32,
    )
    scale_now = 1.0 / math.sqrt(HD)
    d_queries = (
        jnp.einsum("hqk,khe->qhe", d_scores, key_heads, preferred_element_type=jnp.float32)
        * scale_now
    )
    d_keys = (
        jnp.einsum("hqk,qhe->khe", d_scores, query_heads, preferred_element_type=jnp.float32)
        * scale_now
    )
    stacked = jnp.stack([d_queries, d_keys, d_values]).reshape(3, seq_len, queries.shape[1])
    return stacked.astype(jnp.bfloat16)


def per_device(inputs, w_qkv, w_out, w_up, w_down, norm_gains, biases, up_bias, cotangent):
    qkv_cols, out_rows, up_cols, down_rows = (
        lax.all_gather(w_qkv, "fsdp", axis=1, tiled=True),
        lax.all_gather(w_out, "fsdp", axis=1, tiled=True),
        lax.all_gather(w_up, "fsdp", axis=0, tiled=True),
        lax.all_gather(w_down, "fsdp", axis=1, tiled=True),
    )
    qkv_whole, out_whole, up_whole = (
        lax.all_gather(qkv_cols, "tp", axis=2, tiled=True),
        lax.all_gather(out_rows, "tp", axis=0, tiled=True),
        lax.all_gather(up_cols, "tp", axis=1, tiled=True),
    )
    local_cols = qkv_cols.shape[2]
    tp_index = lax.axis_index("tp")
    col_start = tp_index * local_cols
    residual = inputs.astype(jnp.float32)
    normed_one, unit_one, inv_std_one = norm_forward(residual, norm_gains[0], biases[0])
    gathered_one = lax.all_gather(normed_one.astype(jnp.bfloat16), "tp", axis=1, tiled=True)
    projected = jnp.einsum(
        "bsd,cde->cbse", gathered_one, qkv_cols, preferred_element_type=jnp.float32
    )
    queries = (projected[0] + lax.dynamic_slice_in_dim(biases[1], col_start, local_cols)).astype(
        jnp.bfloat16
    )
    key_rows = projected[1].astype(jnp.bfloat16)
    values = (projected[2] + lax.dynamic_slice_in_dim(biases[2], col_start, local_cols)).astype(
        jnp.bfloat16
    )
    mixed_out, log_totals = lax.map(attend_forward, (queries, key_rows, values))
    mixed_block = lax.all_to_all(mixed_out, "tp", split_axis=1, concat_axis=2, tiled=True)
    attn_rows = jnp.einsum(
        "bse,ed->bsd", mixed_block, out_whole, preferred_element_type=jnp.float32
    )
    middle = residual + attn_rows + biases[3]
    normed_two, unit_two, inv_std_two = norm_forward(middle, norm_gains[1], biases[4])
    normed_two = normed_two.astype(jnp.bfloat16)
    upstream = cotangent.astype(jnp.float32)
    gathered_two = lax.all_gather(normed_two, "tp", axis=1, tiled=True)
    unit_count = up_cols.shape[1]
    unit_start = tp_index * unit_count
    pre_act = jnp.einsum("bsd,df->bsf", gathered_two, up_cols, preferred_element_type=jnp.float32)
    pre_act = pre_act + lax.dynamic_slice_in_dim(up_bias, unit_start, unit_count)
    activated = gelu_tanh(pre_act).astype(jnp.bfloat16)
    unit_terms = jnp.einsum("bsf,fd->bsd", activated, down_rows, preferred_element_type=jnp.float32)
    mlp_rows = lax.psum_scatter(
        unit_terms.astype(jnp.bfloat16), "tp", scatter_dimension=1, tiled=True
    ).astype(jnp.float32)
    grad_rows = lax.all_gather(cotangent, "tp", axis=1, tiled=True)
    d_down = jnp.einsum("bsf,bsd->fd", activated, grad_rows, preferred_element_type=jnp.float32)
    d_act = jnp.einsum("bsd,fd->bsf", grad_rows, down_rows, preferred_element_type=jnp.float32)
    d_pre = (d_act * gelu_slope(pre_act)).astype(jnp.bfloat16)
    d_up = jnp.einsum("bsd,bsf->df", gathered_two, d_pre, preferred_element_type=jnp.float32)
    up_bias_grad = lax.dynamic_update_slice_in_dim(
        jnp.zeros(up_bias.shape, jnp.float32),
        jnp.sum(d_pre, axis=(0, 1), dtype=jnp.float32),
        unit_start,
        0,
    )
    pre_block = lax.all_to_all(d_pre, "tp", split_axis=1, concat_axis=2, tiled=True)
    d_normed_two = jnp.einsum(
        "bsf,df->bsd", pre_block, up_whole, preferred_element_type=jnp.float32
    )
    outputs = (middle + mlp_rows + biases[5]).astype(jnp.bfloat16)
    d_middle_norm, gain_two_grad, shift_two_grad = norm_backward(
        d_normed_two, unit_two, inv_std_two, norm_gains[1]
    )
    d_middle = upstream + d_middle_norm
    grad_branch = lax.all_gather(d_middle.astype(jnp.bfloat16), "tp", axis=1, tiled=True)
    d_out = jnp.einsum("bse,bsd->ed", mixed_out, grad_branch, preferred_element_type=jnp.float32)
    d_mixed = jnp.einsum(
        "bsd,ed->bse", grad_branch, out_rows, preferred_element_type=jnp.float32
    ).astype(jnp.bfloat16)
    d_qkv = lax.map(attend_backward, (queries, key_rows, values, log_totals, d_mixed))
    d_qkv_weight = jnp.einsum(
        "bsd,bcse->cde", gathered_one, d_qkv, preferred_element_type=jnp.float32
    )
    qkv_bias_grad = jnp.sum(d_qkv, axis=(0, 2), dtype=jnp.float32)
    qkv_block = lax.all_to_all(d_qkv, "tp", split_axis=2, concat_axis=3, tiled=True)
    d_normed_one = jnp.einsum(
        "bcse,cde->bsd", qkv_block, qkv_whole, preferred_element_type=jnp.float32
    )
    d_input_norm, gain_one_grad, shift_one_grad = norm_backward(
        d_normed_one, unit_one, inv_std_one, norm_gains[0]
    )
    input_grad = d_middle + d_input_norm
    qkv_grad, out_grad, up_grad, down_grad = (
        lax.psum_scatter(
            d_qkv_weight.astype(jnp.bfloat16), "fsdp", scatter_dimension=1, tiled=True
        ).astype(jnp.float32),
        lax.psum_scatter(
            d_out.astype(jnp.bfloat16), "fsdp", scatter_dimension=1, tiled=True
        ).astype(jnp.float32),
        lax.psum_scatter(d_up.astype(jnp.bfloat16), "fsdp", scatter_dimension=0, tiled=True).astype(
            jnp.float32
        ),
        lax.psum_scatter(
            d_down.astype(jnp.bfloat16), "fsdp", scatter_dimension=1, tiled=True
        ).astype(jnp.float32),
    )
    blank_row = jnp.zeros((biases.shape[1],), jnp.float32)
    query_bias_grad = lax.dynamic_update_slice_in_dim(blank_row, qkv_bias_grad[0], col_start, 0)
    value_bias_grad = lax.dynamic_update_slice_in_dim(blank_row, qkv_bias_grad[2], col_start, 0)
    bias_rows = jnp.stack(
        [
            shift_one_grad,
            query_bias_grad,
            value_bias_grad,
            jnp.sum(d_middle, axis=(0, 1)),
            shift_two_grad,
            jnp.sum(upstream, axis=(0, 1)),
        ]
    )
    gain_rows = jnp.stack([gain_one_grad, gain_two_grad])
    gain_total, bias_total, up_total = lax.psum(
        (gain_rows, bias_rows, up_bias_grad), ("fsdp", "tp")
    )
    return (
        outputs,
        input_grad,
        qkv_grad,
        out_grad,
        up_grad,
        down_grad,
        gain_total,
        bias_total,
        up_total,
    )


def solution(mesh):
    return jax.shard_map(
        per_device,
        mesh=mesh,
        in_specs=(
            P("fsdp", "tp", None),
            P(None, "fsdp", "tp"),
            P("tp", "fsdp"),
            P("fsdp", "tp"),
            P("tp", "fsdp"),
            P(),
            P(),
            P(),
            P("fsdp", "tp", None),
        ),
        out_specs=(
            P("fsdp", "tp", None),
            P("fsdp", "tp", None),
            P(None, "fsdp", "tp"),
            P("tp", "fsdp"),
            P("fsdp", "tp"),
            P("tp", "fsdp"),
            P(),
            P(),
            P(),
        ),
        check_vma=False,
    )
```

profile of v0, /device:TPU:0, one launch (start us, length us, event | category | flops | bytes accessed | tf_op | source)
XLA Modules:
  0.0 1260.8 jit_solution(792191084101287380)
XLA Ops:
  17.6 34.6 %all-gather.16.cloned.1.call-done = bf16[576,1152]{0,1:T(8,128)(2,1)} async-done(((bf16[576,72]{0,1:T(8,128)(2,1)}), bf16[576,1152]{0,1:T(8,128)(2,1)}) %all-gather.16.cloned.1.call-update) | async-done | bytes 1327120 | tf_op jit(solution)/shard_map/all_gather | solution.py:109
  55.6 45.3 %all-gather.12.cloned.1.call-done = bf16[2,736,1152]{2,1,0:T(8,128)(2,1)} async-done(((bf16[2,368,1152]{2,1,0:T(8,128)(2,1)}), bf16[2,736,1152]{2,1,0:T(8,128)(2,1)}) %all-gather.12.cloned.1.call-update) | async-done | bytes 3391504 | tf_op jit(solution)/shard_map/all_gather | solution.py:123
  100.9 54.0 %all-gather.14.cloned.1.call-done = bf16[3,1152,576]{2,1,0:T(8,128)(2,1)} async-done(((bf16[3,72,576]{2,1,0:T(8,128)(2,1)}), bf16[3,1152,576]{2,1,0:T(8,128)(2,1)}) %all-gather.14.cloned.1.call-update) | async-done | bytes 3981328 | tf_op jit(solution)/shard_map/all_gather | solution.py:108
  167.1 70.3 %while.22 = (s32[]{:T(128)}, bf16[2,736,576]{1,2,0:T(8,128)(2,1)}, f32[2,8,736]{2,1,0:T(8,128)}, bf16[2,736,576]{1,2,0:T(8,128)(2,1)S(1)}, bf16[2,736,576]{1,2,0...) while((s32[]{:T(128)}, bf16[2,736,576]{1,2,0:T(8,128)(2,1)}, f32[2,8,736]{2,1,0:T(8,128)}, ...), condition=%wide.region_5.6_spmd, body=%wide.region_2.5_spmd.sunk | while | flops 1300489216 | bytes 76576920 | solution.py:134
  244.2 29.1 %all_to_all.54 = bf16[2,736,576]{2,0,1:T(2,128)(2,1)} all-to-all(bf16[2,736,576]{2,0,1:T(2,128)(2,1)} %copy.67), channel_id=1, replica_groups=mesh['fsdp'=16,'tp'=2] {'tp'}, dimensions={1} | all-to-all | bytes 3391488 | tf_op jit(solution)/shard_map/all_to_all | solution.py:135
  298.9 34.5 %all-gather.20.cloned.1.call-done = bf16[2,736,1152]{2,1,0:T(8,128)(2,1)} async-done(((bf16[2,368,1152]{2,1,0:T(8,128)(2,1)}), bf16[2,736,1152]{2,1,0:T(8,128)(2,1)}) %all-gather.20.cloned.1.call-update) | async-done | bytes 3391504 | tf_op jit(solution)/shard_map/all_gather | solution.py:143
  333.4 14.6 %fusion.32 = f32[2,736,2152]{2,1,0:T(8,128)} fusion(bf16[2,736,1152]{2,1,0:T(8,128)(2,1)} %all-gather.20.cloned.1.call-done, bf16[1152,2152]{1,0:T(8,128)(2,1)} %all-gather.22.cloned.1.call-done), kind=kOutput, calls=%fused_computation.62 | convolution fusion | flops 7298482176 | bytes 21020672 | tf_op jit(solution)/shard_map/bsd,df->bsf/dot_general | solution.py:146
  348.0 42.5 %all-gather.24.cloned.1.call-done = bf16[2152,1152]{0,1:T(8,128)(2,1)} async-done(((bf16[2152,72]{0,1:T(8,128)(2,1)}), bf16[2152,1152]{0,1:T(8,128)(2,1)}) %all-gather.24.cloned.1.call-update) | async-done | bytes 4958224 | tf_op jit(solution)/shard_map/all_gather | solution.py:111
  390.5 16.8 %fusion.34 = bf16[2,736,1152]{2,1,0:T(8,128)(2,1)} fusion(bf16[2152,1152]{0,1:T(8,128)(2,1)} %all-gather.24.cloned.1.call-done, f32[2,736,2152]{2,1,0:T(8,128)} %fusion.32, f32[2152]{0:T(1024)S(1)} %dynamic_slice.37), kind=kOutput, calls=%fused_computation.64 | convolution fusion | flops 7331855360 | bytes 21029280 | tf_op jit(solution)/shard_map/bsf,fd->bsd/dot_general | solution.py:149
  407.4 30.9 %all-gather.26.cloned.1.call-done = bf16[2,736,1152]{2,1,0:T(8,128)(2,1)} async-done(((bf16[2,368,1152]{2,1,0:T(8,128)(2,1)}), bf16[2,736,1152]{2,1,0:T(8,128)(2,1)}) %all-gather.26.cloned.1.call-update) | async-done | bytes 3391504 | tf_op jit(solution)/shard_map/all_gather | solution.py:153
  438.3 18.3 %convert_reduce_fusion = (f32[2152]{0:T(1024)}, bf16[2,736,2152]{2,1,0:T(8,128)(2,1)S(1)}) fusion(f32[2,736,2152]{2,1,0:T(8,128)} %fusion.32, f32[2152]{0:T(1024)S(1)} %dynamic_slice.37, bf16[2,736,1152]{2,1,0:T(8,128)(2,1)} %all-gather.26.cloned.1.call-done, bf16[2152,1152]{0,1:T(8,128)(2,1)} %all-gather.24.cloned.1.call-done), kind=kOutput, calls=%fused_computation.45 | convolution fusion | flops 7368170496 | bytes 27373376 | tf_op jit(solution)/shard_map/bsd,fd->bsf/dot_general | solution.py:155
  465.2 143.9 %all_to_all.55 = bf16[2,736,2152]{2,0,1:T(2,128)(2,1)S(1)} all-to-all(bf16[2,736,2152]{2,0,1:T(2,128)(2,1)S(1)} %copy.71), channel_id=1, replica_groups=mesh['fsdp'=16,'tp'=2] {'tp'}, dimensions={1} | all-to-all | bytes 12670976 | tf_op jit(solution)/shard_map/all_to_all | solution.py:164
  631.8 15.6 %multiply_reduce_fusion.1 = (f32[1152]{0:T(1024)}, f32[2,368]{1,0:T(2,128)S(1)}, f32[2,368]{1,0:T(2,128)S(1)}, f32[1152]{0:T(1024)}, f32[2,368,1152]{2,1,0:T(8,128)}) fusion(f32[2,368,1152]{2,1,0:T(8,128)S(1)} %get-tuple-element.182, f32[2,368]{1,0:T(2,128)S(1)} %add_rsqrt_fusion, f32[2,368]{1,0:T(2,128)S(1)} %broadcast_multiply_fusion.4, ...), kind=kOutput, calls=%fused_computation.97 | convolution fusion | flops 7306109952 | bytes 23060480 | tf_op jit(solution)/shard_map/bsf,df->bsd/dot_general | solution.py:165
  647.4 32.6 %reduce-scatter.11.cloned.1.call-done = bf16[2,368,1152]{2,1,0:T(8,128)(2,1)} async-done(((bf16[2,736,1152]{2,1,0:T(8,128)(2,1)}), bf16[2,368,1152]{2,1,0:T(8,128)(2,1)}) %reduce-scatter.11.cloned.1.call-update) | async-done | bytes 1695760 | tf_op jit(solution)/shard_map/reduce_scatter | solution.py:150
  689.2 14.9 %fusion.24 = bf16[2152,1152]{0,1:T(8,128)(2,1)} fusion(bf16[2,736,1152]{2,1,0:T(8,128)(2,1)S(1)} %copy-done.33, f32[2,736,2152]{2,1,0:T(8,128)} %fusion.32, f32[2152]{0:T(1024)S(1)} %dynamic_slice.37), kind=kOutput, calls=%fused_computation.48 | convolution fusion | flops 7332638720 | bytes 21029280 | tf_op jit(solution)/shard_map/bsf,bsd->fd/dot_general | solution.py:154
  719.0 17.4 %all-gather.30.cloned.1.call-done = bf16[2,736,1152]{2,1,0:T(8,128)(2,1)} async-done(((bf16[2,368,1152]{2,1,0:T(8,128)(2,1)}), bf16[2,736,1152]{2,1,0:T(8,128)(2,1)}) %all-gather.30.cloned.1.call-update) | async-done | bytes 3391504 | tf_op jit(solution)/shard_map/all_gather | solution.py:173
  742.6 109.6 %while.23 = (s32[]{:T(128)}, bf16[2,3,736,576]{2,3,1,0:T(8,128)(2,1)}, bf16[2,736,576]{1,2,0:T(8,128)(2,1)S(1)}, bf16[2,736,576]{1,2,0:T(8,128)(2,1)}, f32[2,8,7...) while((s32[]{:T(128)}, ...), condition=%wide.region_13.14_spmd, body=%wide.region_11.13_spmd.sunk | while | flops 3194917888 | bytes 150634480 | solution.py:178
  831.4 14.6 %multiply_convert_fusion.9 = bf16[8,736,736]{1,2,0:T(8,128)(2,1)S(1)} fusion(f32[8,736,736]{1,2,0:T(8,128)} %get-tuple-element.287, f32[8,736,736]{1,2,0:T(8,128)} %fusion.133, f32[8,736]{1,0:T(8,128)S(1)} %get-tuple-element.288, f32[8,736]{1,0:T(8,128)S(1)} %dynamic-slice_bitcast_fusion.2, pred[736]{0:T(1024)(128)(4,1)S(1)} %iota_compare_fusion.5), kind=kLoop, calls=%fused_computation.15.clone.1 | loop fusion | flops 26001408 | bytes 43383520 | tf_op jit(solution)/shard_map/while/body/eval_jaxpr/convert_element_type | solution.py:86
  889.5 18.0 %copy.74 = bf16[2,3,736,576]{3,0,1,2:T(2,128)(2,1)} copy(bf16[2,3,736,576]{2,3,1,0:T(8,128)(2,1)} %get-tuple-element.81) | data formatting | bytes 10174464 | tf_op jit(solution)/shard_map/while | solution.py:178
  923.1 112.5 %all-reduce.7.cloned.1.call-done = bf16[3,1152,576]{2,0,1:T(4,128)(2,1)} async-done(((bf16[3,1152,576]{2,0,1:T(4,128)(2,1)}), bf16[3,1152,576]{2,0,1:T(4,128)(2,1)}) %all-reduce.7.cloned.1.call-update) | async-done | bytes 3981328
  1037.5 60.6 %reduce-scatter.13.cloned.1.call-done = bf16[576,72]{0,1:T(8,128)(2,1)} async-done(((bf16[576,1152]{0,1:T(8,128)(2,1)}), bf16[576,72]{0,1:T(8,128)(2,1)}) %reduce-scatter.13.cloned.1.call-update) | async-done | bytes 82960
  1099.7 18.2 %copy.75 = bf16[2,3,2,368,576]{3,4,2,1,0:T(8,128)(2,1)} copy(bf16[2,3,2,368,576]{4,0,1,3,2:T(2,128)(2,1)} %bitcast.34) | data formatting | bytes 10174464 | tf_op jit(solution)/shard_map/all_to_all | solution.py:183
  1117.8 79.9 %all-gather.32.cloned.1.call-done = bf16[3,1152,1152]{1,2,0:T(8,128)(2,1)} async-done(((bf16[3,1152,576]{1,2,0:T(8,128)(2,1)}), bf16[3,1152,1152]{1,2,0:T(8,128)(2,1)}) %all-gather.32.cloned.1.call-update) | async-done | bytes 7962640 | tf_op jit(solution)/shard_map/all_gather | solution.py:114
  1212.8 41.2 %all-reduce.4 = (f32[2,1152]{1,0:T(2,128)}, f32[6,1152]{1,0:T(8,128)}, f32[4304]{0:T(1024)}) all-reduce(f32[2,1152]{1,0:T(2,128)S(1)} %pad_maximum_fusion, f32[6,1152]{1,0:T(8,128)S(1)} %stack.45, f32[4304]{0:T(1024)S(1)} %dynamic_update_slice.25), channel_id=1, replica_groups=mesh['fsdp'=16,'tp'=2] {'fsdp','tp'}, use_global_device_ids=true, to_apply=%region_22.23 | all-reduce | flops 13520 | bytes 108160 | tf_op jit(solution)/shard_map/psum | solution.py:219
  (221 shorter events, 354.7 us)
Async XLA Ops:
  7.2 45.1 %all-gather.16.cloned.1.call-start = ((), (), s32[]{:S(2)}) async-start(), calls=%async_computation.9 | async-start | bytes 1566720 | tf_op jit(solution)/shard_map/all_gather | solution.py:109
  7.9 93.0 %all-gather.12.cloned.1.call-start = ((), (), s32[]{:S(2)}) async-start(), calls=%async_computation.7 | async-start | bytes 5087232 | tf_op jit(solution)/shard_map/all_gather | solution.py:123
  16.8 138.1 %all-gather.14.cloned.1.call-start = ((), (), s32[]{:S(2)}) async-start(), calls=%async_computation.8 | async-start | bytes 4700160 | tf_op jit(solution)/shard_map/all_gather | solution.py:108
  17.6 262.3 %all-gather.18.cloned.1.call-start = ((), (), s32[]{:S(2)}) async-start(), calls=%async_computation.10 | async-start | bytes 3981312 | tf_op jit(solution)/shard_map/all_gather | solution.py:115
  54.9 234.6 %all-gather.22.cloned.1.call-start = ((), (), s32[]{:S(2)}) async-start(), calls=%async_computation.12 | async-start | bytes 5326848 | tf_op jit(solution)/shard_map/all_gather | solution.py:110
  55.5 277.9 %all-gather.20.cloned.1.call-start = ((), (), s32[]{:S(2)}) async-start(), calls=%async_computation.11 | async-start | bytes 5087232 | tf_op jit(solution)/shard_map/all_gather | solution.py:143
  237.4 42.4 %copy-start = (bf16[2,736,576]{1,2,0:T(8,128)(2,1)}, bf16[2,736,576]{1,2,0:T(8,128)(2,1)S(1)}, u32[]{:S(2)}) copy-start(bf16[2,736,576]{1,2,0:T(8,128)(2,1)S(1)} %get-tuple-element.350) | copy-start | bytes 5087236
  237.4 42.4 %copy-start.2 = (bf16[2,736,576]{1,2,0:T(8,128)(2,1)}, bf16[2,736,576]{1,2,0:T(8,128)(2,1)S(1)}, u32[]{:S(2)}) copy-start(bf16[2,736,576]{1,2,0:T(8,128)(2,1)S(1)} %get-tuple-element.351) | copy-start | bytes 5087236
  287.9 102.6 %all-gather.24.cloned.1.call-start = ((), (), s32[]{:S(2)}) async-start(), calls=%async_computation.13 | async-start | bytes 5326848 | tf_op jit(solution)/shard_map/all_gather | solution.py:111
  288.6 149.7 %all-gather.26.cloned.1.call-start = ((), (), s32[]{:S(2)}) async-start(), calls=%async_computation.15 | async-start | bytes 5087232 | tf_op jit(solution)/shard_map/all_gather | solution.py:153
  289.4 342.4 %all-gather.28.cloned.1.call-start = ((), (), s32[]{:S(2)}) async-start(), calls=%async_computation.16 | async-start | bytes 14874624 | tf_op jit(solution)/shard_map/all_gather | solution.py:116
  298.1 381.9 %reduce-scatter.11.cloned.1.call-start = ((), (), s32[]{:S(2)}) async-start(), calls=%async_computation.14 | async-start | bytes 5087232 | tf_op jit(solution)/shard_map/reduce_scatter | solution.py:150
  407.3 329.1 %all-gather.30.cloned.1.call-start = ((), (), s32[]{:S(2)}) async-start(), calls=%async_computation.17 | async-start | bytes 5087232 | tf_op jit(solution)/shard_map/all_gather | solution.py:173
  631.2 48.8 %copy-start.22 = (f32[1152]{0:T(1024)S(1)}, f32[1152]{0:T(1024)}, u32[]{:S(2)}) copy-start(f32[1152]{0:T(1024)} %get-tuple-element.126) | copy-start | bytes 13828
  688.6 227.0 %reduce-scatter.17.cloned.1.call-start = ((), (), s32[]{:S(2)}) async-start(), calls=%async_computation.22 | async-start | bytes 5326848
  704.1 213.3 %reduce-scatter.15.cloned.1.call-start = ((), (), s32[]{:S(2)}) async-start(), calls=%async_computation.21 | async-start | bytes 5326848
  719.0 316.7 %all-reduce.7.cloned.1.call-start = ((), (), s32[]{:S(2)}) async-start(), calls=%async_computation.19 | async-start | bytes 11796480
  875.2 222.9 %reduce-scatter.13.cloned.1.call-start = ((), (), s32[]{:S(2)}) async-start(), calls=%async_computation.20 | async-start | bytes 1566720
  882.8 314.9 %all-gather.32.cloned.1.call-start = ((), (), s32[]{:S(2)}) async-start(), calls=%async_computation.18 | async-start | bytes 11943936 | tf_op jit(solution)/shard_map/all_gather | solution.py:114
  907.5 192.2 %all-to-all-start.2 = ((bf16[2,3,736,576]{3,0,1,2:T(2,128)(2,1)}), bf16[2,3,736,576]{3,0,1,2:T(2,128)(2,1)}, u32[]{:S(2)}, u32[]{:S(2)}) async-start(bf16[2,3,736,576]{3,0,1,2:T(2,128)(2,1)} %copy.74), calls=%async_computation.3 | async-start | bytes 11304960 | tf_op jit(solution)/shard_map/all_to_all | solution.py:183
  1099.7 98.1 %copy-start.5 = (bf16[2,368,1152]{2,1,0:T(8,128)(2,1)S(1)}, bf16[2,368,1152]{2,1,0:T(8,128)(2,1)}, u32[]{:S(2)}) copy-start(bf16[2,368,1152]{2,1,0:T(8,128)(2,1)} %param.13) | copy-start | bytes 5087236
  1099.7 98.1 %copy-start.18 = (f32[1152]{0:T(1024)S(1)}, f32[1152]{0:T(1024)}, u32[]{:S(2)}) copy-start(f32[1152]{0:T(1024)} %copy-done.17) | copy-start | bytes 13828
  1099.7 98.1 %copy-start.21 = (f32[2,368]{1,0:T(2,128)S(1)}, f32[2,368]{1,0:T(2,128)}, u32[]{:S(2)}) copy-start(f32[2,368]{1,0:T(2,128)} %copy-done.20) | copy-start | bytes 8836
  1099.7 98.1 %copy-start.27 = (f32[2,368]{1,0:T(2,128)S(1)}, f32[2,368]{1,0:T(2,128)}, u32[]{:S(2)}) copy-start(f32[2,368]{1,0:T(2,128)} %copy-done.26) | copy-start | bytes 8836
  (34 other events, 299.7 us)
Sparse Core Ops, SparseCore 0:
  10.2 42.0 all-gather.15
  54.4 46.5 all-gather.11
  103.1 51.7 all-gather.13
  156.3 37.8 all-gather.17
  196.2 54.9 all-gather.21
  288.0 45.2 all-gather.19
  335.5 54.9 all-gather.23
  392.0 46.2 all-gather.25
  439.9 191.8 all-gather.27
  633.9 46.0 reduce-scatter.10
  688.7 47.6 all-gather.29
  740.3 77.9 reduce-scatter.16
  822.8 76.9 reduce-scatter.14
  903.4 132.1 all-reduce.6
  1039.2 58.7 reduce-scatter.12
  1099.5 98.1 all-gather.31
where the time goes:
time: 1270 us; the launch traced here: 1260 us
  waiting for transfers between devices  549 us (43%)
  matrix products  257 us (20%)
  blocking collectives  214 us (17%)
  local copies, waits for them, and re-layouts  136 us (11%)
  other arithmetic  81 us (6%)
  between operations  15.3 us (1%)
    unnamed x20, waiting for transfers between devices  177 us
    all_to_all x1, blocking collectives, per_device(): lax.all_to_all(d_pre, 'tp', split_axis=1, concat_axis=2, tiled=True)  144 us
    all_gather x1, waiting for transfers between devices, per_device(): lax.all_gather(qkv_cols, 'tp', axis=2, tiled=True)  79.9 us
    all_gather x1, waiting for transfers between devices, per_device(): lax.all_gather(w_qkv, 'fsdp', axis=1, tiled=True)  54 us
    all_gather x1, waiting for transfers between devices, per_device(): lax.all_gather(normed_one.astype(jnp.bfloat16), 'tp', axis=1, tiled=True)  45.3 us
    all_gather x1, waiting for transfers between devices, per_device(): lax.all_gather(w_down, 'fsdp', axis=1, tiled=True)  42.5 us
    psum x1, blocking collectives, per_device(): lax.psum((gain_rows, bias_rows, up_bias_grad), ('fsdp', 'tp'))  41.2 us
    dot_general x4, matrix products, masked_scores(): jnp.einsum('qhe,khe->hqk', query_heads, key_heads, preferred_element_type...  36.4 us
  transfers between devices with their start and end apart: 17, of which 12 were waited for; matrix products, arithmetic and copies ran while one was open for 34% of the time, Pallas kernels for 0%

commit v1 on v0

v1 whole, which is shorter than its diff:
```python
import math

import jax
import jax.numpy as jnp
from jax import lax
from jax.sharding import PartitionSpec as P

HD = 72
VALID = 729


norm_eps = 1e-06
gelu_coef = math.sqrt(2.0 / math.pi)


def norm_forward(values, scale_row, shift_row):
    average = jnp.mean(values, axis=-1, keepdims=True)
    centred = values - average
    inv_std = lax.rsqrt(jnp.mean(centred * centred, axis=-1, keepdims=True) + norm_eps)
    normed = centred * inv_std
    return (normed * scale_row + shift_row, normed, inv_std)


def norm_backward(upstream, normed, inv_std, scale_row):
    scaled = upstream * scale_row
    back = inv_std * (
        scaled
        - jnp.mean(scaled, axis=-1, keepdims=True)
        - normed * jnp.mean(scaled * normed, axis=-1, keepdims=True)
    )
    return (back, jnp.sum(upstream * normed, axis=0), jnp.sum(upstream, axis=0))


def gelu_tanh(pre_act):
    return (
        0.5
        * pre_act
        * (1.0 + jnp.tanh(gelu_coef * (pre_act + 0.044715 * pre_act * pre_act * pre_act)))
    )


def gelu_slope(pre_act):
    tangent = jnp.tanh(gelu_coef * (pre_act + 0.044715 * pre_act * pre_act * pre_act))
    inner_slope = gelu_coef * (1.0 + 3.0 * 0.044715 * pre_act * pre_act)
    return 0.5 * (1.0 + tangent) + 0.5 * pre_act * (1.0 - tangent * tangent) * inner_slope


def masked_scores(queries, key_rows, positions):
    seq_len = queries.shape[0]
    head_count = queries.shape[1] // HD
    query_heads = queries.reshape(seq_len, head_count, HD)
    key_heads = key_rows.reshape(seq_len, head_count, HD)
    scores = jnp.einsum("qhe,khe->hqk", query_heads, key_heads, preferred_element_type=jnp.float32)
    scores = scores * (1.0 / math.sqrt(HD))
    visible = (positions < VALID)[None, None, :]
    return (jnp.where(visible, scores, -1e30), query_heads, key_heads)


def attend_forward(queries, key_rows, values, positions):
    seq_len = queries.shape[0]
    scores, query_heads, key_heads = masked_scores(queries, key_rows, positions)
    value_heads = values.reshape(seq_len, -1, HD)
    largest = jnp.max(scores, axis=-1, keepdims=True)
    powers = jnp.exp(scores - largest)
    summed = jnp.sum(powers, axis=-1, keepdims=True)
    attn_probs = (powers / summed).astype(jnp.bfloat16)
    mixed_out = jnp.einsum(
        "hqk,khe->qhe", attn_probs, value_heads, preferred_element_type=jnp.float32
    )
    log_totals = (largest + jnp.log(summed))[:, :, 0]
    return (mixed_out.reshape(seq_len, queries.shape[1]).astype(jnp.bfloat16), log_totals)


def attend_backward(queries, key_rows, values, log_totals, d_mixed, positions):
    seq_len = queries.shape[0]
    scores, query_heads, key_heads = masked_scores(queries, key_rows, positions)
    value_heads = values.reshape(seq_len, -1, HD)
    grad_heads = d_mixed.reshape(seq_len, -1, HD)
    probs_full = jnp.exp(scores - log_totals[:, :, None])
    d_probs = jnp.einsum(
        "qhe,khe->hqk", grad_heads, value_heads, preferred_element_type=jnp.float32
    )
    row_inner = jnp.sum(probs_full * d_probs, axis=-1, keepdims=True)
    d_scores = (probs_full * (d_probs - row_inner)).astype(jnp.bfloat16)
    d_values = jnp.einsum(
        "hqk,qhe->khe",
        probs_full.astype(jnp.bfloat16),
        grad_heads,
        preferred_element_type=jnp.float32,
    )
    scale_now = 1.0 / math.sqrt(HD)
    d_queries = (
        jnp.einsum("hqk,khe->qhe", d_scores, key_heads, preferred_element_type=jnp.float32)
        * scale_now
    )
    d_keys = (
        jnp.einsum("hqk,qhe->khe", d_scores, query_heads, preferred_element_type=jnp.float32)
        * scale_now
    )
    parts = [d_queries, d_keys, d_values]
    return jnp.concatenate(
        [part.reshape(seq_len, queries.shape[1]).astype(jnp.bfloat16) for part in parts], axis=1
    )


def dot(left, right, dims):
    return lax.dot_general(left, right, (dims, ((), ())), preferred_element_type=jnp.float32)


ROWS_COLS = ((1,), (0,))
ROWS_ROWS = ((1,), (1,))
COLS_COLS = ((0,), (0,))


def swap_halves(block):
    return lax.ppermute(block, "tp", [(0, 1), (1, 0)])


def gather_rows(block):
    if lax.axis_size("tp") == 2:
        return jnp.concatenate([block, swap_halves(block)], axis=0)
    return lax.all_gather(block, "tp", axis=0, tiled=True)


def scatter_dot(left, right, dims):
    if lax.axis_size("tp") == 2:
        half = left.shape[0] // 2
        away = swap_halves(dot(left[half:], right, dims).astype(jnp.bfloat16))
        return dot(left[:half], right, dims) + away.astype(jnp.float32)
    return lax.psum_scatter(
        dot(left, right, dims).astype(jnp.bfloat16), "tp", scatter_dimension=0, tiled=True
    ).astype(jnp.float32)


def gather_weight(shard):
    return lax.all_gather(shard, "fsdp", axis=0, tiled=True)


def scatter_weight(whole):
    return lax.psum_scatter(
        whole.astype(jnp.bfloat16), "fsdp", scatter_dimension=0, tiled=True
    ).astype(jnp.float32)


def per_device(inputs, w_qkv, w_out, w_up, w_down, norm_gains, biases, up_bias, cotangent):
    image_count, rows_here, width = inputs.shape
    images = range(image_count)
    local_cols = w_qkv.shape[2]
    unit_count = w_up.shape[1]
    shard_rows = w_qkv.shape[1]
    tp_index = lax.axis_index("tp")
    seq_len = rows_here * lax.axis_size("tp")
    col_start = tp_index * local_cols
    unit_start = tp_index * unit_count
    positions = lax.iota(jnp.int32, seq_len)
    if lax.axis_size("tp") == 2:
        positions = positions + tp_index * rows_here
        positions = jnp.where(positions >= seq_len, positions - seq_len, positions)

    qkv_all = gather_weight(w_qkv.transpose(1, 0, 2).reshape(shard_rows, 3 * local_cols))
    out_all = gather_weight(w_out.T)
    up_all = gather_weight(w_up)
    down_all = gather_weight(w_down.T)
    query_bias = lax.dynamic_slice_in_dim(biases[1], col_start, local_cols)
    value_bias = lax.dynamic_slice_in_dim(biases[2], col_start, local_cols)
    unit_bias = lax.dynamic_slice_in_dim(up_bias, unit_start, unit_count)
    qkv_bias = jnp.concatenate([query_bias, jnp.zeros_like(query_bias), value_bias])

    residual = [inputs[i].astype(jnp.float32) for i in images]
    first = [norm_forward(residual[i], norm_gains[0], biases[0]) for i in images]
    gathered_one = [gather_rows(first[i][0].astype(jnp.bfloat16)) for i in images]
    grad_rows = [gather_rows(cotangent[i]) for i in images]

    saved, mixed, middle, second, gathered_two = [], [], [], [], []
    for i in images:
        projected = (dot(gathered_one[i], qkv_all, ROWS_COLS) + qkv_bias).astype(jnp.bfloat16)
        queries, key_rows, values = (
            projected[:, c * local_cols : (c + 1) * local_cols] for c in range(3)
        )
        mixed_out, log_totals = attend_forward(queries, key_rows, values, positions)
        saved.append((queries, key_rows, values, log_totals))
        mixed.append(mixed_out)
        middle.append(residual[i] + scatter_dot(mixed_out, out_all, ROWS_ROWS) + biases[3])
        second.append(norm_forward(middle[i], norm_gains[1], biases[4]))
        gathered_two.append(gather_rows(second[i][0].astype(jnp.bfloat16)))

    activated, d_pre, outputs, d_normed_two = [], [], [], []
    for i in images:
        pre_act = dot(gathered_two[i], up_all, ROWS_COLS) + unit_bias
        activated.append(gelu_tanh(pre_act).astype(jnp.bfloat16))
        d_act = dot(grad_rows[i], down_all, ROWS_COLS)
        d_pre.append((d_act * gelu_slope(pre_act)).astype(jnp.bfloat16))
        d_normed_two.append(scatter_dot(d_pre[i], up_all, ROWS_ROWS))
        mlp_rows = scatter_dot(activated[i], down_all, ROWS_ROWS)
        outputs.append((middle[i] + mlp_rows + biases[5]).astype(jnp.bfloat16))

    def joined(parts):
        return jnp.concatenate(parts, axis=0)

    grads_whole, units_whole = joined(grad_rows), joined(d_pre)
    down_grad = scatter_weight(dot(grads_whole, joined(activated), COLS_COLS)).T
    up_grad = scatter_weight(dot(joined(gathered_two), units_whole, COLS_COLS))
    unit_sums = jnp.sum(units_whole, axis=0, dtype=jnp.float32)

    gain_two, shift_two, d_middle, branch = [], [], [], []
    for i in images:
        back, gain_part, shift_part = norm_backward(
            d_normed_two[i], second[i][1], second[i][2], norm_gains[1]
        )
        gain_two.append(gain_part)
        shift_two.append(shift_part)
        d_middle.append(cotangent[i].astype(jnp.float32) + back)
        branch.append(gather_rows(d_middle[i].astype(jnp.bfloat16)))

    d_qkv, d_normed_one = [], []
    for i in images:
        d_mixed = dot(branch[i], out_all, ROWS_COLS).astype(jnp.bfloat16)
        d_qkv.append(attend_backward(*saved[i], d_mixed, positions))
        d_normed_one.append(scatter_dot(d_qkv[i], qkv_all, ROWS_ROWS))
    out_grad = scatter_weight(dot(joined(branch), joined(mixed), COLS_COLS)).T
    qkv_whole = joined(d_qkv)
    qkv_grad = scatter_weight(dot(joined(gathered_one), qkv_whole, COLS_COLS))
    qkv_grad = qkv_grad.reshape(shard_rows, 3, local_cols).transpose(1, 0, 2)
    qkv_sums = jnp.sum(qkv_whole, axis=0, dtype=jnp.float32)

    input_grad, gain_one, shift_one = [], [], []
    for i in images:
        back, gain_part, shift_part = norm_backward(
            d_normed_one[i], first[i][1], first[i][2], norm_gains[0]
        )
        gain_one.append(gain_part)
        shift_one.append(shift_part)
        input_grad.append(d_middle[i] + back)

    blank_row = jnp.zeros((width,), jnp.float32)
    query_sums = lax.dynamic_update_slice_in_dim(blank_row, qkv_sums[:local_cols], col_start, 0)
    value_sums = lax.dynamic_update_slice_in_dim(blank_row, qkv_sums[2 * local_cols :], col_start, 0)
    unit_row = lax.dynamic_update_slice_in_dim(jnp.zeros_like(up_bias), unit_sums, unit_start, 0)
    out_sums = sum(jnp.sum(d_middle[i], axis=0) for i in images)
    top_sums = jnp.sum(cotangent, axis=(0, 1), dtype=jnp.float32)
    pieces = [
        sum(gain_one), sum(shift_one), query_sums, value_sums,
        sum(gain_two), sum(shift_two), out_sums, top_sums, unit_row,
    ]
    total = lax.psum(jnp.concatenate(pieces), ("fsdp", "tp"))
    rows = total[: 8 * width].reshape(8, width)
    gain_total = jnp.stack([rows[0], rows[4]])
    bias_total = jnp.stack([rows[1], rows[2], rows[3], rows[6], rows[5], rows[7]])
    return (
        jnp.stack(outputs),
        jnp.stack(input_grad),
        qkv_grad,
        out_grad,
        up_grad,
        down_grad,
        gain_total,
        bias_total,
        total[8 * width :],
    )


def solution(mesh):
    return jax.shard_map(
        per_device,
        mesh=mesh,
        in_specs=(
            P("fsdp", "tp", None),
            P(None, "fsdp", "tp"),
            P("tp", "fsdp"),
            P("fsdp", "tp"),
            P("tp", "fsdp"),
            P(),
            P(),
            P(),
            P("fsdp", "tp", None),
        ),
        out_specs=(
            P("fsdp", "tp", None),
            P("fsdp", "tp", None),
            P(None, "fsdp", "tp"),
            P("tp", "fsdp"),
            P("fsdp", "tp"),
            P("tp", "fsdp"),
            P(),
            P(),
            P(),
        ),
        check_vma=False,
    )
```

time: 1270 us -> 655 us (0.52)
  waiting for transfers between devices: 549 us -> 204 us
  blocking collectives: 214 us -> 40.5 us
  local copies, waits for them, and re-layouts: 136 us -> 36.1 us
    all_gather x11 -> x4, waiting for transfers between devices: 340 us -> 25.5 us  [gather_weight(): return lax.all_gather(shard, 'fsdp', axis=0, tiled=True)]
    unnamed x20 -> x11, waiting for transfers between devices: 177 us -> 1.48 us
    all_to_all x2 -> x0, blocking collectives: 173 us -> none  [the longest x1 144 us: per_device(): lax.all_to_all(d_pre, 'tp', split_axis=1, concat_axis=2, tiled=True)]
    ppermute x0 -> x16, waiting for transfers between devices: none -> 135 us  [swap_halves(): return lax.ppermute(block, 'tp', [(0, 1), (1, 0)])]
    all_to_all x4 -> x0, local copies, waits for them, and re-layouts: 46.8 us -> none  [the longest x2 22 us: per_device(): lax.all_to_all(d_pre, 'tp', split_axis=1, concat_axis=2, tiled=True)]
    while x26 -> x0, local copies, waits for them, and re-layouts: 28.2 us -> none  [the longest x1 18 us: per_device(): lax.map(attend_backward, (queries, key_rows, values, log_totals, d_mixed))]
    convert_element_type x3 -> x0, local copies, waits for them, and re-layouts: 20.1 us -> none  [the longest x1 11.3 us: per_device(): d_qkv_weight.astype(jnp.bfloat16)]
    all_gather x3 -> x0, local copies, waits for them, and re-layouts: 17.8 us -> none  [the longest x1 8.6 us: per_device(): lax.all_gather(w_up, 'fsdp', axis=0, tiled=True)]
  transfers between devices with their start and end apart: 17 -> 24, of which waited for: 12 -> 11; matrix products, arithmetic and copies ran while one was open for 34% -> 54% of each run, Pallas kernels for 0% -> 0%
where the time goes in v1:
time: 655 us; the launch traced here: 650 us
  matrix products  251 us (38%)
  waiting for transfers between devices  204 us (31%)
  other arithmetic  85 us (13%)
  blocking collectives  40.5 us (6%)
  local copies, waits for them, and re-layouts  36.1 us (6%)
  starting transfers between devices  17.3 us (3%)
  between operations  15.7 us (2%)
    dot_general x28, matrix products, dot(): lax.dot_general(left, right, (dims, ((), ())), preferred_element_type=jnp...  163 us
    ppermute x16, waiting for transfers between devices, swap_halves(): return lax.ppermute(block, 'tp', [(0, 1), (1, 0)])  135 us
    reduce_scatter x1, waiting for transfers between devices, scatter_weight(): lax.psum_scatter(whole.astype(jnp.bfloat16), 'fsdp', scatter_dimension=0,...  41.2 us
    psum x1, blocking collectives, per_device(): total = lax.psum(jnp.concatenate(pieces), ('fsdp', 'tp'))  40.5 us
    convert_element_type x2, other arithmetic, attend_backward(): d_scores = (probs_full * (d_probs - row_inner)).astype(jnp.bfloat16)  25.9 us
    all_gather x4, waiting for transfers between devices, gather_weight(): return lax.all_gather(shard, 'fsdp', axis=0, tiled=True)  25.5 us
    dot_general x2, matrix products, attend_backward(): jnp.einsum('qhe,khe->hqk', grad_heads, value_heads, preferred_element_typ...  24 us
    dot_general x2, matrix products, attend_backward(): jnp.einsum('hqk,qhe->khe', probs_full.astype(jnp.bfloat16), grad_heads, p...  19.7 us
  transfers between devices with their start and end apart: 24, of which 11 were waited for; matrix products, arithmetic and copies ran while one was open for 54% of the time, Pallas kernels for 0%

profile of v1, /device:TPU:0, one launch (start us, length us, event | category | flops | bytes accessed | tf_op | source)
XLA Modules:
  0.0 649.6 jit_solution(3423712494130585117)
XLA Ops:
  18.9 19.4 %collective-permute-done.4 = bf16[368,1152]{1,0:T(8,128)(2,1)} collective-permute-done((bf16[368,1152]{1,0:T(8,128)(2,1)S(1)}, bf16[368,1152]{1,0:T(8,128)(2,1)}, u32[]{:S(2)}, u32[]{:S(2)}) %collective-permute-start.4) | collective-permute-done | bytes 847904 | tf_op jit(solution)/shard_map/ppermute | solution.py:116
  38.4 25.5 %all-gather.5.cloned.1.call-done = bf16[1152,1728]{1,0:T(8,128)(2,1)} async-done(((bf16[72,1728]{1,0:T(8,128)(2,1)}), bf16[1152,1728]{1,0:T(8,128)(2,1)}) %all-gather.5.cloned.1.call-update) | async-done | bytes 3981328 | tf_op jit(solution)/shard_map/all_gather | solution.py:136
  93.1 9.6 %fusion.204 = (f32[8,736]{1,0:T(8,128)S(1)}, f32[8,736,736]{1,2,0:T(8,128)}) fusion(bf16[736,8,72]{0,2,1:T(8,128)(2,1)} %bitcast.205, bf16[736,8,72]{0,2,1:T(8,128)(2,1)S(1)} %bitcast.195, pred[736]{0:T(1024)(128)(4,1)S(1)} %fusion.180), kind=kOutput, calls=%fused_computation.287 | convolution fusion | flops 637028608 | bytes 19054304 | tf_op jit(solution)/shard_map/qhe,khe->hqk/dot_general | solution.py:53
  156.8 19.2 %collective-permute-done.5 = bf16[368,1152]{1,0:T(8,128)(2,1)S(1)} collective-permute-done((bf16[368,1152]{1,0:T(8,128)(2,1)S(1)}, bf16[368,1152]{1,0:T(8,128)(2,1)S(1)}, u32[]{:S(2)}, u32[]{:S(2)}) %collective-permute-start.5) | collective-permute-done | bytes 847904 | tf_op jit(solution)/shard_map/ppermute | solution.py:116
  185.5 17.8 %collective-permute-done.6 = bf16[368,1152]{1,0:T(8,128)(2,1)} collective-permute-done((bf16[368,1152]{1,0:T(8,128)(2,1)}, bf16[368,1152]{1,0:T(8,128)(2,1)}, u32[]{:S(2)}, u32[]{:S(2)}) %collective-permute-start.6) | collective-permute-done | bytes 847904 | tf_op jit(solution)/shard_map/ppermute | solution.py:116
  203.3 10.3 %fusion.112 = f32[736,2152]{1,0:T(8,128)} fusion(bf16[1152,2152]{1,0:T(8,128)(2,1)} %all-gather.9.cloned.1.call-done, bf16[368,1152]{1,0:T(8,128)(2,1)} %collective-permute-done.6, bf16[368,1152]{1,0:T(8,128)(2,1)} %get-tuple-element.94), kind=kOutput, calls=%fused_computation.155 | convolution fusion | flops 3652632576 | bytes 12989440 | tf_op jit(solution)/shard_map/dot_general | solution.py:107
  213.6 26.0 %collective-permute-done.12 = bf16[368,1152]{1,0:T(8,128)(2,1)} collective-permute-done((bf16[368,1152]{1,0:T(8,128)(2,1)S(1)}, bf16[368,1152]{1,0:T(8,128)(2,1)}, u32[]{:S(2)}, u32[]{:S(2)}) %collective-permute-start.12) | collective-permute-done | bytes 847904 | tf_op jit(solution)/shard_map/ppermute | solution.py:116
  239.6 11.1 %fusion.27 = bf16[736,2152]{1,0:T(8,128)(2,1)S(1)} fusion(bf16[1152,2152]{1,0:T(8,128)(2,1)} %all-gather.11.cloned.1.call-done, f32[736,2152]{1,0:T(8,128)} %fusion.112, f32[2152]{0:T(1024)S(1)} %dynamic_slice.17, bf16[368,1152]{1,0:T(8,128)(2,1)} %collective-permute-done.12, bf16[368,1152]{1,0:T(8,128)(2,1)S(1)} %get-tuple-element.78), kind=kOutput, calls=%fused_computation.46 | convolution fusion | flops 3684310016 | bytes 16165792 | tf_op jit(solution)/shard_map/dot_general | solution.py:107
  257.8 11.5 %multiply_convert_fusion.3 = (bf16[736,2152]{1,0:T(8,128)(2,1)}, bf16[736,2152]{1,0:T(8,128)(2,1)}, f32[736,2152]{1,0:T(8,128)}) fusion(f32[2152]{0:T(1024)S(1)} %dynamic_slice.17, f32[736,2152]{1,0:T(8,128)} %fusion.112, bf16[1152,2152]{1,0:T(8,128)(2,1)S(1)} %copy-done.73, bf16[368,1152]{1,0:T(8,128)(2,1)} %collective-permute-done.2, ...), kind=kOutput, calls=%fused_computation.52 | convolution fusion | flops 3684310016 | bytes 25669024 | tf_op jit(solution)/shard_map/dot_general | solution.py:107
  269.3 9.6 %fusion.21 = bf16[736,2152]{1,0:T(8,128)(2,1)S(1)} fusion(bf16[1152,2152]{1,0:T(8,128)(2,1)S(1)} %bitcast.236, f32[736,2152]{1,0:T(8,128)} %get-tuple-element.105, f32[2152]{0:T(1024)S(1)} %dynamic_slice.17, bf16[368,1152]{1,0:T(8,128)(2,1)} %collective-permute-done.8, bf16[368,1152]{1,0:T(8,128)(2,1)S(1)} %get-tuple-element.77), kind=kOutput, calls=%fused_computation.40 | convolution fusion | flops 3684310016 | bytes 16165792 | tf_op jit(solution)/shard_map/dot_general | solution.py:107
  284.4 14.1 %collective-permute-done.9 = bf16[368,1152]{1,0:T(8,128)(2,1)S(1)} collective-permute-done((bf16[368,1152]{1,0:T(8,128)(2,1)S(1)}, bf16[368,1152]{1,0:T(8,128)(2,1)S(1)}, u32[]{:S(2)}, u32[]{:S(2)}) %collective-permute-start.9) | collective-permute-done | bytes 847904 | tf_op jit(solution)/shard_map/ppermute | solution.py:116
  308.4 19.8 %collective-permute-done.14 = bf16[368,1152]{1,0:T(8,128)(2,1)S(1)} collective-permute-done((bf16[368,1152]{1,0:T(8,128)(2,1)S(1)}, bf16[368,1152]{1,0:T(8,128)(2,1)S(1)}, u32[]{:S(2)}, u32[]{:S(2)}) %collective-permute-start.14) | collective-permute-done | bytes 847904 | tf_op jit(solution)/shard_map/ppermute | solution.py:116
  328.2 12.6 %collective-permute-done.10 = bf16[368,1152]{1,0:T(8,128)(2,1)S(1)} collective-permute-done((bf16[368,1152]{1,0:T(8,128)(2,1)S(1)}, bf16[368,1152]{1,0:T(8,128)(2,1)S(1)}, u32[]{:S(2)}, u32[]{:S(2)}) %collective-permute-start.10) | collective-permute-done | bytes 847904 | tf_op jit(solution)/shard_map/ppermute | solution.py:116
  346.4 14.3 %convolution_convert_fusion.1 = bf16[1152,2152]{1,0:T(8,128)(2,1)} fusion(bf16[736,2152]{1,0:T(8,128)(2,1)} %copy-done.24, bf16[736,2152]{1,0:T(8,128)(2,1)} %copy-done.25, bf16[368,1152]{1,0:T(8,128)(2,1)} %collective-permute-done.6, bf16[368,1152]{1,0:T(8,128)(2,1)} %get-tuple-element.94, bf16[368,1152]{1,0:T(8,128)(2,1)} %collective-permute-done.2, ...), kind=kOutput, calls=%fused_computation.18 | convolution fusion | flops 7327198208 | bytes 14685184 | tf_op jit(solution)/shard_map/dot_general | solution.py:107
  377.7 13.0 %convolution_convert_fusion = bf16[1152,2152]{1,0:T(8,128)(2,1)} fusion(bf16[736,2152]{1,0:T(8,128)(2,1)S(1)} %copy-done.83, bf16[736,2152]{1,0:T(8,128)(2,1)S(1)} %copy-done.81, bf16[368,1152]{1,0:T(8,128)(2,1)} %collective-permute-done.12, bf16[368,1152]{1,0:T(8,128)(2,1)S(1)} %copy-done.38, bf16[368,1152]{1,0:T(8,128)(2,1)} %collective-permute-done.8, ...), kind=kOutput, calls=%fused_computation.17 | convolution fusion | flops 7327198208 | bytes 14685184 | tf_op jit(solution)/shard_map/dot_general | solution.py:107
  412.5 10.2 %fusion.161 = bf16[8,72,736]{2,1,0:T(8,128)(2,1)S(1)} fusion(bf16[736,8,72]{0,2,1:T(8,128)(2,1)S(1)} %bitcast.221, f32[8,736,736]{1,2,0:T(8,128)} %get-tuple-element.104, f32[8,736]{1,0:T(8,128)S(1)} %log_add_fusion), kind=kOutput, calls=%fused_computation.213 | convolution fusion | flops 633124864 | bytes 19053568 | tf_op jit(solution)/shard_map/hqk,qhe->khe/dot_general | solution.py:85
  422.7 12.4 %multiply_reduce_fusion = (f32[8,736]{1,0:T(8,128)S(1)}, f32[8,736,736]{1,2,0:T(8,128)}) fusion(f32[8,736,736]{1,2,0:T(8,128)} %get-tuple-element.104, f32[8,736]{1,0:T(8,128)S(1)} %log_add_fusion, bf16[736,8,72]{0,2,1:T(8,128)(2,1)S(1)} %bitcast.222, bf16[736,8,72]{0,2,1:T(8,128)(2,1)S(1)} %bitcast.218), kind=kOutput, calls=%fused_computation.1 | convolution fusion | flops 637028608 | bytes 36411392 | tf_op jit(solution)/shard_map/qhe,khe->hqk/dot_general | solution.py:80
  435.0 12.9 %multiply_convert_fusion = bf16[8,736,736]{1,2,0:T(8,128)(2,1)S(1)} fusion(f32[8,736,736]{1,2,0:T(8,128)} %get-tuple-element.110, f32[8,736,736]{1,2,0:T(8,128)} %get-tuple-element.104, f32[8,736]{1,0:T(8,128)S(1)} %get-tuple-element.109, f32[8,736]{1,0:T(8,128)S(1)} %log_add_fusion), kind=kLoop, calls=%fused_computation | loop fusion | flops 17334272 | bytes 43382784 | tf_op jit(solution)/shard_map/convert_element_type | solution.py:84
  461.1 11.6 %multiply_reduce_fusion.1 = (f32[8,736]{1,0:T(8,128)S(1)}, f32[8,736,736]{1,2,0:T(8,128)}) fusion(f32[8,736,736]{1,2,0:T(8,128)} %get-tuple-element.102, f32[8,736]{1,0:T(8,128)S(1)} %log_add_fusion.1, bf16[736,8,72]{0,2,1:T(8,128)(2,1)S(1)} %bitcast.219, bf16[736,8,72]{0,2,1:T(8,128)(2,1)S(1)} %bitcast.216), kind=kOutput, calls=%fused_computation.4 | convolution fusion | flops 637028608 | bytes 36411392 | tf_op jit(solution)/shard_map/qhe,khe->hqk/dot_general | solution.py:80
  472.7 13.0 %multiply_convert_fusion.1 = bf16[8,736,736]{1,2,0:T(8,128)(2,1)S(1)} fusion(f32[8,736,736]{1,2,0:T(8,128)} %get-tuple-element.108, f32[8,736,736]{1,2,0:T(8,128)} %get-tuple-element.102, f32[8,736]{1,0:T(8,128)S(1)} %get-tuple-element.107, f32[8,736]{1,0:T(8,128)S(1)} %log_add_fusion.1), kind=kLoop, calls=%fused_computation.3 | loop fusion | flops 17334272 | bytes 43382784 | tf_op jit(solution)/shard_map/convert_element_type | solution.py:84
  506.1 12.6 %convolution_convert_fusion.2 = bf16[1152,1728]{1,0:T(8,128)(2,1)} fusion(bf16[368,1152]{1,0:T(8,128)(2,1)} %collective-permute-done.4, bf16[368,1152]{1,0:T(8,128)(2,1)} %copy-done.45, bf16[368,1152]{1,0:T(8,128)(2,1)} %collective-permute-done, bf16[368,1152]{1,0:T(8,128)(2,1)} %copy-done.44, bf16[736,576]{0,1:T(8,128)(2,1)S(1)} %bitcast.210, ...), kind=kOutput, calls=%fused_computation.30 | convolution fusion | flops 5906571264 | bytes 12460032 | tf_op jit(solution)/shard_map/dot_general | solution.py:107
  518.7 13.3 %convert_reduce_fusion.1 = f32[1728]{0:T(1024)S(1)} fusion(bf16[736,576]{0,1:T(8,128)(2,1)} %bitcast.211, bf16[736,576]{0,1:T(8,128)(2,1)S(1)} %bitcast.201, bf16[736,576]{0,1:T(8,128)(2,1)S(1)} %bitcast.191, bf16[736,576]{0,1:T(8,128)(2,1)} %bitcast.214, bf16[736,576]{0,1:T(8,128)(2,1)S(1)} %bitcast.204, bf16[736,576]{0,1:T(8,128)(2,1)S(1)} %bitcast.194), kind=kLoop, calls=%fused_computation.19 | loop fusion | flops 33065280 | bytes 5094144 | tf_op jit(solution)/shard_map/reduce_sum | solution.py:224
  545.1 40.5 %psum.7 = f32[13520]{0:T(1024)S(1)} all-reduce(f32[13520]{0:T(1024)S(1)} %constant_dynamic-update-slice_fusion), channel_id=1, replica_groups=mesh['fsdp'=16,'tp'=2] {'fsdp','tp'}, use_global_device_ids=true, to_apply=%region_39.40 | all-reduce | flops 13520 | bytes 108160 | tf_op jit(solution)/shard_map/psum | solution.py:245
  599.3 41.2 %reduce-scatter.11.cloned.1.call-done = bf16[72,1728]{1,0:T(8,128)(2,1)} async-done(((bf16[1152,1728]{1,0:T(8,128)(2,1)}), bf16[72,1728]{1,0:T(8,128)(2,1)}) %reduce-scatter.11.cloned.1.call-update) | async-done | bytes 248848 | tf_op jit(solution)/shard_map/reduce_scatter | solution.py:140
  (337 shorter events, 232.6 us)
Async XLA Ops:
  7.2 56.7 %all-gather.5.cloned.1.call-start = ((), (), s32[]{:S(2)}) async-start(), calls=%async_computation.4 | async-start | bytes 4386816 | tf_op jit(solution)/shard_map/all_gather | solution.py:136
  9.4 112.9 %all-gather.7.cloned.1.call-start = ((), (), s32[]{:S(2)}) async-start(), calls=%async_computation.5 | async-start | bytes 1566720 | tf_op jit(solution)/shard_map/all_gather | solution.py:136
  10.2 193.1 %all-gather.9.cloned.1.call-start = ((), (), s32[]{:S(2)}) async-start(), calls=%async_computation.6 | async-start | bytes 5326848 | tf_op jit(solution)/shard_map/all_gather | solution.py:136
  10.9 228.7 %all-gather.11.cloned.1.call-start = ((), (), s32[]{:S(2)}) async-start(), calls=%async_computation.7 | async-start | bytes 5326848 | tf_op jit(solution)/shard_map/all_gather | solution.py:136
  15.5 22.8 %collective-permute-start.4 = (bf16[368,1152]{1,0:T(8,128)(2,1)S(1)}, bf16[368,1152]{1,0:T(8,128)(2,1)}, u32[]{:S(2)}, u32[]{:S(2)}) collective-permute-start(bf16[368,1152]{1,0:T(8,128)(2,1)S(1)} %get-tuple-element.70), channel_id=1, source_target_pairs={{0,1},{1,0},{2,3},{3,2},{4,5},{5,4},{6,7},{7,6},{8,9},{9,8},{10,11... | collective-permute-start | bytes 2543624 | tf_op jit(solution)/shard_map/ppermute | solution.py:116
  18.6 60.0 %collective-permute-start = (bf16[368,1152]{1,0:T(8,128)(2,1)S(1)}, bf16[368,1152]{1,0:T(8,128)(2,1)}, u32[]{:S(2)}, u32[]{:S(2)}) collective-permute-start(bf16[368,1152]{1,0:T(8,128)(2,1)S(1)} %get-tuple-element.69), channel_id=1, source_target_pairs={{0,1},{1,0},{2,3},{3,2},{4,5},{5,4},{6,7},{7,6},{8,9},{9,8},{10,11... | collective-permute-start | bytes 2543624 | tf_op jit(solution)/shard_map/ppermute | solution.py:116
  18.7 575.3 %reduce-scatter.13.cloned.1.call-start = ((), (), s32[]{:S(2)}) async-start(), calls=%async_computation.9 | async-start | bytes 1566720
  125.8 31.0 %collective-permute-start.1 = (bf16[368,1152]{1,0:T(8,128)(2,1)}, bf16[368,1152]{1,0:T(8,128)(2,1)}, u32[]{:S(2)}, u32[]{:S(2)}) collective-permute-start(bf16[368,1152]{1,0:T(8,128)(2,1)} %convolution_convert_fusion.10), channel_id=1, source_target_pairs={{0,1},{1,0},{2,3},{3,2},{4,5},{5,4},{6,7},{7,6},{8,9},{9,8},{10,11... | collective-permute-start | bytes 2543624 | tf_op jit(solution)/shard_map/ppermute | solution.py:116
  155.3 20.7 %collective-permute-start.5 = (bf16[368,1152]{1,0:T(8,128)(2,1)S(1)}, bf16[368,1152]{1,0:T(8,128)(2,1)S(1)}, u32[]{:S(2)}, u32[]{:S(2)}) collective-permute-start(bf16[368,1152]{1,0:T(8,128)(2,1)S(1)} %convolution_convert_fusion.8), channel_id=1, source_target_pairs={{0,1},{1,0},{2,3},{3,2},{4,5},{5,4},{6,7},{7,6},{8,9},{9,8},{10,11... | collective-permute-start | bytes 2543624 | tf_op jit(solution)/shard_map/ppermute | solution.py:116
  181.2 22.1 %collective-permute-start.6 = (bf16[368,1152]{1,0:T(8,128)(2,1)}, bf16[368,1152]{1,0:T(8,128)(2,1)}, u32[]{:S(2)}, u32[]{:S(2)}) collective-permute-start(bf16[368,1152]{1,0:T(8,128)(2,1)} %get-tuple-element.94), channel_id=1, source_target_pairs={{0,1},{1,0},{2,3},{3,2},{4,5},{5,4},{6,7},{7,6},{8,9},{9,8},{10,11... | collective-permute-start | bytes 2543624 | tf_op jit(solution)/shard_map/ppermute | solution.py:116
  181.9 87.4 %collective-permute-start.8 = (bf16[368,1152]{1,0:T(8,128)(2,1)S(1)}, bf16[368,1152]{1,0:T(8,128)(2,1)}, u32[]{:S(2)}, u32[]{:S(2)}) collective-permute-start(bf16[368,1152]{1,0:T(8,128)(2,1)S(1)} %get-tuple-element.77), channel_id=1, source_target_pairs={{0,1},{1,0},{2,3},{3,2},{4,5},{5,4},{6,7},{7,6},{8,9},{9,8},{10,11... | collective-permute-start | bytes 2543624 | tf_op jit(solution)/shard_map/ppermute | solution.py:116
  183.4 56.2 %collective-permute-start.12 = (bf16[368,1152]{1,0:T(8,128)(2,1)S(1)}, bf16[368,1152]{1,0:T(8,128)(2,1)}, u32[]{:S(2)}, u32[]{:S(2)}) collective-permute-start(bf16[368,1152]{1,0:T(8,128)(2,1)S(1)} %get-tuple-element.78), channel_id=1, source_target_pairs={{0,1},{1,0},{2,3},{3,2},{4,5},{5,4},{6,7},{7,6},{8,9},{9,8},{10,11... | collective-permute-start | bytes 2543624 | tf_op jit(solution)/shard_map/ppermute | solution.py:116
  184.1 73.7 %collective-permute-start.2 = (bf16[368,1152]{1,0:T(8,128)(2,1)}, bf16[368,1152]{1,0:T(8,128)(2,1)}, u32[]{:S(2)}, u32[]{:S(2)}) collective-permute-start(bf16[368,1152]{1,0:T(8,128)(2,1)} %get-tuple-element.93), channel_id=1, source_target_pairs={{0,1},{1,0},{2,3},{3,2},{4,5},{5,4},{6,7},{7,6},{8,9},{9,8},{10,11... | collective-permute-start | bytes 2543624 | tf_op jit(solution)/shard_map/ppermute | solution.py:116
  253.1 28.9 %collective-permute-start.13 = (bf16[368,1152]{1,0:T(8,128)(2,1)S(1)}, bf16[368,1152]{1,0:T(8,128)(2,1)S(1)}, u32[]{:S(2)}, u32[]{:S(2)}) collective-permute-start(bf16[368,1152]{1,0:T(8,128)(2,1)S(1)} %convolution_convert_fusion.5), channel_id=1, source_target_pairs={{0,1},{1,0},{2,3},{3,2},{4,5},{5,4},{6,7},{7,6},{8,9},{9,8},{10,11... | collective-permute-start | bytes 2543624 | tf_op jit(solution)/shard_map/ppermute | solution.py:116
  281.4 17.2 %collective-permute-start.9 = (bf16[368,1152]{1,0:T(8,128)(2,1)S(1)}, bf16[368,1152]{1,0:T(8,128)(2,1)S(1)}, u32[]{:S(2)}, u32[]{:S(2)}) collective-permute-start(bf16[368,1152]{1,0:T(8,128)(2,1)S(1)} %convolution_convert_fusion.6), channel_id=1, source_target_pairs={{0,1},{1,0},{2,3},{3,2},{4,5},{5,4},{6,7},{7,6},{8,9},{9,8},{10,11... | collective-permute-start | bytes 2543624 | tf_op jit(solution)/shard_map/ppermute | solution.py:116
  306.3 21.9 %collective-permute-start.14 = (bf16[368,1152]{1,0:T(8,128)(2,1)S(1)}, bf16[368,1152]{1,0:T(8,128)(2,1)S(1)}, u32[]{:S(2)}, u32[]{:S(2)}) collective-permute-start(bf16[368,1152]{1,0:T(8,128)(2,1)S(1)} %convert_element_type.282), channel_id=1, source_target_pairs={{0,1},{1,0},{2,3},{3,2},{4,5},{5,4},{6,7},{7,6},{8,9},{9,8},{10,11... | collective-permute-start | bytes 2543624 | tf_op jit(solution)/shard_map/ppermute | solution.py:116
  307.2 33.5 %collective-permute-start.10 = (bf16[368,1152]{1,0:T(8,128)(2,1)S(1)}, bf16[368,1152]{1,0:T(8,128)(2,1)S(1)}, u32[]{:S(2)}, u32[]{:S(2)}) collective-permute-start(bf16[368,1152]{1,0:T(8,128)(2,1)S(1)} %convert_element_type.263), channel_id=1, source_target_pairs={{0,1},{1,0},{2,3},{3,2},{4,5},{5,4},{6,7},{7,6},{8,9},{9,8},{10,11... | collective-permute-start | bytes 2543624 | tf_op jit(solution)/shard_map/ppermute | solution.py:116
  346.4 249.2 %reduce-scatter.15.cloned.1.call-start = ((), (), s32[]{:S(2)}) async-start(), calls=%async_computation.10 | async-start | bytes 5326848
  360.8 236.7 %reduce-scatter.17.cloned.1.call-start = ((), (), s32[]{:S(2)}) async-start(), calls=%async_computation.11 | async-start | bytes 5326848
  369.6 25.8 %collective-permute-start.7 = (bf16[368,1152]{1,0:T(8,128)(2,1)}, bf16[368,1152]{1,0:T(8,128)(2,1)}, u32[]{:S(2)}, u32[]{:S(2)}) collective-permute-start(bf16[368,1152]{1,0:T(8,128)(2,1)} %convolution_convert_fusion.7), channel_id=1, source_target_pairs={{0,1},{1,0},{2,3},{3,2},{4,5},{5,4},{6,7},{7,6},{8,9},{9,8},{10,11... | collective-permute-start | bytes 2543624 | tf_op jit(solution)/shard_map/ppermute | solution.py:116
  376.7 26.8 %collective-permute-start.3 = (bf16[368,1152]{1,0:T(8,128)(2,1)}, bf16[368,1152]{1,0:T(8,128)(2,1)}, u32[]{:S(2)}, u32[]{:S(2)}) collective-permute-start(bf16[368,1152]{1,0:T(8,128)(2,1)} %convolution_convert_fusion.9), channel_id=1, source_target_pairs={{0,1},{1,0},{2,3},{3,2},{4,5},{5,4},{6,7},{7,6},{8,9},{9,8},{10,11... | collective-permute-start | bytes 2543624 | tf_op jit(solution)/shard_map/ppermute | solution.py:116
  394.9 245.6 %reduce-scatter.11.cloned.1.call-start = ((), (), s32[]{:S(2)}) async-start(), calls=%async_computation.8 | async-start | bytes 4386816 | tf_op jit(solution)/shard_map/reduce_scatter | solution.py:140
  458.1 74.4 %collective-permute-start.15 = (bf16[368,1152]{1,0:T(8,128)(2,1)}, bf16[368,1152]{1,0:T(8,128)(2,1)}, u32[]{:S(2)}, u32[]{:S(2)}) collective-permute-start(bf16[368,1152]{1,0:T(8,128)(2,1)} %convolution_convert_fusion.3), channel_id=1, source_target_pairs={{0,1},{1,0},{2,3},{3,2},{4,5},{5,4},{6,7},{7,6},{8,9},{9,8},{10,11... | collective-permute-start | bytes 2543624 | tf_op jit(solution)/shard_map/ppermute | solution.py:116
  505.9 31.8 %collective-permute-start.11 = (bf16[368,1152]{1,0:T(8,128)(2,1)}, bf16[368,1152]{1,0:T(8,128)(2,1)}, u32[]{:S(2)}, u32[]{:S(2)}) collective-permute-start(bf16[368,1152]{1,0:T(8,128)(2,1)} %convolution_convert_fusion.4), channel_id=1, source_target_pairs={{0,1},{1,0},{2,3},{3,2},{4,5},{5,4},{6,7},{7,6},{8,9},{9,8},{10,11... | collective-permute-start | bytes 2543624 | tf_op jit(solution)/shard_map/ppermute | solution.py:116
  (86 other events, 1521.2 us)
Sparse Core Ops, SparseCore 0:
  10.9 52.9 all-gather.4
  66.0 37.8 all-gather.6
  106.0 53.7 all-gather.8
  161.8 53.4 all-gather.10
  346.5 56.7 reduce-scatter.12
  407.2 76.9 reduce-scatter.14
  488.8 76.9 reduce-scatter.16
  569.7 70.7 reduce-scatter.10

commit v2 on v1

--- a/solution.py
+++ b/solution.py
@@ -138,8 +138,12 @@
 
 def scatter_weight(whole):
     return lax.psum_scatter(
-        whole.astype(jnp.bfloat16), "fsdp", scatter_dimension=0, tiled=True
+        whole.astype(jnp.bfloat16), "fsdp", scatter_dimension=0, tiled=False
     ).astype(jnp.float32)
+
+
+def by_shard(whole):
+    return whole.astype(jnp.bfloat16).reshape(lax.axis_size("fsdp"), -1, whole.shape[1])
 
 
 def per_device(inputs, w_qkv, w_out, w_up, w_down, norm_gains, biases, up_bias, cotangent):
@@ -198,8 +202,13 @@
         return jnp.concatenate(parts, axis=0)
 
     grads_whole, units_whole = joined(grad_rows), joined(d_pre)
-    down_grad = scatter_weight(dot(grads_whole, joined(activated), COLS_COLS)).T
-    up_grad = scatter_weight(dot(joined(gathered_two), units_whole, COLS_COLS))
+    down_whole = by_shard(dot(grads_whole, joined(activated), COLS_COLS))
+    up_whole = by_shard(dot(joined(gathered_two), units_whole, COLS_COLS))
+    down_whole, up_whole, d_normed_two = lax.optimization_barrier(
+        (down_whole, up_whole, d_normed_two)
+    )
+    down_grad = scatter_weight(down_whole).T
+    up_grad = scatter_weight(up_whole)
     unit_sums = jnp.sum(units_whole, axis=0, dtype=jnp.float32)
 
     gain_two, shift_two, d_middle, branch = [], [], [], []
@@ -217,9 +226,9 @@
         d_mixed = dot(branch[i], out_all, ROWS_COLS).astype(jnp.bfloat16)
         d_qkv.append(attend_backward(*saved[i], d_mixed, positions))
         d_normed_one.append(scatter_dot(d_qkv[i], qkv_all, ROWS_ROWS))
-    out_grad = scatter_weight(dot(joined(branch), joined(mixed), COLS_COLS)).T
+    out_grad = scatter_weight(by_shard(dot(joined(branch), joined(mixed), COLS_COLS))).T
     qkv_whole = joined(d_qkv)
-    qkv_grad = scatter_weight(dot(joined(gathered_one), qkv_whole, COLS_COLS))
+    qkv_grad = scatter_weight(by_shard(dot(joined(gathered_one), qkv_whole, COLS_COLS)))
     qkv_grad = qkv_grad.reshape(shard_rows, 3, local_cols).transpose(1, 0, 2)
     qkv_sums = jnp.sum(qkv_whole, axis=0, dtype=jnp.float32)
 

time: 655 us -> 747 us (1.14)
  waiting for transfers between devices: 204 us -> 264 us
  local copies, waits for them, and re-layouts: 36.1 us -> 58.3 us
  other arithmetic: 85 us -> 96.3 us
    unnamed x11, waiting for transfers between devices: 1.48 us -> 120 us
    reduce_scatter x1, waiting for transfers between devices: 41.2 us -> 0.01 us  [scatter_weight(): lax.psum_scatter(whole.astype(jnp.bfloat16), 'fsdp', scatter_dimension=0,...]
    convert_element_type x0 -> x4, local copies, waits for them, and re-layouts: none -> 26.2 us  [by_shard(): whole.astype(jnp.bfloat16)]
    ppermute x16, waiting for transfers between devices: 135 us -> 119 us  [swap_halves(): return lax.ppermute(block, 'tp', [(0, 1), (1, 0)])]
    reduce_sum x1, other arithmetic: 13.3 us -> 23.4 us  [per_device(): qkv_sums = jnp.sum(qkv_whole, axis=0, dtype=jnp.float32)]
  transfers between devices with their start and end apart: 24 -> 24, of which waited for: 11 -> 11; matrix products, arithmetic and copies ran while one was open for 54% -> 48% of each run, Pallas kernels for 0% -> 0%
where the time goes in v2:
time: 747 us; the launch traced here: 743 us
  waiting for transfers between devices  264 us (35%)
  matrix products  253 us (34%)
  other arithmetic  96.3 us (13%)
  local copies, waits for them, and re-layouts  58.3 us (8%)
  blocking collectives  39.7 us (5%)
  starting transfers between devices  16.3 us (2%)
  between operations  15.7 us (2%)
    dot_general x28, matrix products, dot(): lax.dot_general(left, right, (dims, ((), ())), preferred_element_type=jnp...  163 us
    unnamed x11, waiting for transfers between devices  120 us
    ppermute x16, waiting for transfers between devices, swap_halves(): return lax.ppermute(block, 'tp', [(0, 1), (1, 0)])  119 us
    psum x1, blocking collectives, per_device(): total = lax.psum(jnp.concatenate(pieces), ('fsdp', 'tp'))  39.7 us
    convert_element_type x4, local copies, waits for them, and re-layouts, by_shard(): whole.astype(jnp.bfloat16)  26.2 us
    convert_element_type x2, other arithmetic, attend_backward(): d_scores = (probs_full * (d_probs - row_inner)).astype(jnp.bfloat16)  25.8 us
    all_gather x4, waiting for transfers between devices, gather_weight(): return lax.all_gather(shard, 'fsdp', axis=0, tiled=True)  24.9 us
    dot_general x2, matrix products, attend_backward(): jnp.einsum('qhe,khe->hqk', grad_heads, value_heads, preferred_element_typ...  23.6 us
  transfers between devices with their start and end apart: 24, of which 11 were waited for; matrix products, arithmetic and copies ran while one was open for 48% of the time, Pallas kernels for 0%

profile of v2, /device:TPU:0, one launch (start us, length us, event | category | flops | bytes accessed | tf_op | source)
XLA Modules:
  0.0 743.1 jit_solution(5440039404475208873)
XLA Ops:
  20.4 18.6 %collective-permute-done.4 = bf16[368,1152]{1,0:T(8,128)(2,1)S(1)} collective-permute-done((bf16[368,1152]{1,0:T(8,128)(2,1)S(1)}, bf16[368,1152]{1,0:T(8,128)(2,1)S(1)}, u32[]{:S(2)}, u32[]{:S(2)}) %collective-permute-start.4) | collective-permute-done | bytes 847904 | tf_op jit(solution)/shard_map/ppermute | solution.py:116
  39.0 24.9 %all-gather.5.cloned.1.call-done = bf16[1152,1728]{1,0:T(8,128)(2,1)} async-done(((bf16[72,1728]{1,0:T(8,128)(2,1)}), bf16[1152,1728]{1,0:T(8,128)(2,1)}) %all-gather.5.cloned.1.call-update) | async-done | bytes 3981328 | tf_op jit(solution)/shard_map/all_gather | solution.py:136
  92.1 9.6 %fusion.204 = (f32[8,736]{1,0:T(8,128)}, f32[8,736,736]{1,2,0:T(8,128)}) fusion(bf16[736,8,72]{0,2,1:T(8,128)(2,1)S(1)} %bitcast.221, bf16[736,8,72]{0,2,1:T(8,128)(2,1)S(1)} %bitcast.211, pred[736]{0:T(1024)(128)(4,1)} %fusion.180), kind=kOutput, calls=%fused_computation.288 | convolution fusion | flops 637028608 | bytes 19054304 | tf_op jit(solution)/shard_map/qhe,khe->hqk/dot_general | solution.py:53
  154.8 19.7 %collective-permute-done.5 = bf16[368,1152]{1,0:T(8,128)(2,1)S(1)} collective-permute-done((bf16[368,1152]{1,0:T(8,128)(2,1)S(1)}, bf16[368,1152]{1,0:T(8,128)(2,1)S(1)}, u32[]{:S(2)}, u32[]{:S(2)}) %collective-permute-start.5) | collective-permute-done | bytes 847904 | tf_op jit(solution)/shard_map/ppermute | solution.py:116
  185.2 16.6 %collective-permute-done.6 = bf16[368,1152]{1,0:T(8,128)(2,1)} collective-permute-done((bf16[368,1152]{1,0:T(8,128)(2,1)}, bf16[368,1152]{1,0:T(8,128)(2,1)}, u32[]{:S(2)}, u32[]{:S(2)}) %collective-permute-start.6) | collective-permute-done | bytes 847904 | tf_op jit(solution)/shard_map/ppermute | solution.py:116
  201.7 10.1 %fusion.112 = f32[736,2152]{1,0:T(8,128)} fusion(bf16[1152,2152]{1,0:T(8,128)(2,1)} %all-gather.9.cloned.1.call-done, bf16[368,1152]{1,0:T(8,128)(2,1)} %collective-permute-done.6, bf16[368,1152]{1,0:T(8,128)(2,1)} %get-tuple-element.102), kind=kOutput, calls=%fused_computation.155 | convolution fusion | flops 3652632576 | bytes 12989440 | tf_op jit(solution)/shard_map/dot_general | solution.py:107
  211.9 26.2 %collective-permute-done.9 = bf16[368,1152]{1,0:T(8,128)(2,1)} collective-permute-done((bf16[368,1152]{1,0:T(8,128)(2,1)}, bf16[368,1152]{1,0:T(8,128)(2,1)}, u32[]{:S(2)}, u32[]{:S(2)}) %collective-permute-start.9) | collective-permute-done | bytes 847904 | tf_op jit(solution)/shard_map/ppermute | solution.py:116
  238.1 11.2 %fusion.27 = bf16[736,2152]{1,0:T(8,128)(2,1)S(1)} fusion(bf16[1152,2152]{1,0:T(8,128)(2,1)} %all-gather.11.cloned.1.call-done, f32[736,2152]{1,0:T(8,128)} %fusion.112, f32[2152]{0:T(1024)S(1)} %dynamic_slice.17, bf16[368,1152]{1,0:T(8,128)(2,1)} %collective-permute-done.9, bf16[368,1152]{1,0:T(8,128)(2,1)} %get-tuple-element.86), kind=kOutput, calls=%fused_computation.46 | convolution fusion | flops 3684310016 | bytes 16165792 | tf_op jit(solution)/shard_map/dot_general | solution.py:107
  256.2 11.5 %multiply_convert_fusion.3 = (bf16[736,2152]{1,0:T(8,128)(2,1)}, bf16[736,2152]{1,0:T(8,128)(2,1)}, f32[736,2152]{1,0:T(8,128)}) fusion(f32[2152]{0:T(1024)S(1)} %dynamic_slice.17, f32[736,2152]{1,0:T(8,128)} %fusion.112, bf16[1152,2152]{1,0:T(8,128)(2,1)S(1)} %copy-done.74, bf16[368,1152]{1,0:T(8,128)(2,1)} %collective-permute-done.2, ...), kind=kOutput, calls=%fused_computation.52 | convolution fusion | flops 3684310016 | bytes 25669024 | tf_op jit(solution)/shard_map/dot_general | solution.py:107
  280.8 14.3 %convolution_convert_fusion = bf16[1152,2152]{0,1:T(8,128)(2,1)} fusion(bf16[736,2152]{1,0:T(8,128)(2,1)S(1)} %fusion.27, bf16[736,2152]{1,0:T(8,128)(2,1)S(1)} %fusion.21, bf16[368,1152]{1,0:T(8,128)(2,1)} %collective-permute-done.6, bf16[368,1152]{1,0:T(8,128)(2,1)} %get-tuple-element.102, bf16[368,1152]{1,0:T(8,128)(2,1)} %collective-permute-done.2, ...), kind=kOutput, calls=%fused_computation.17 | convolution fusion | flops 7327198208 | bytes 14685184 | tf_op jit(solution)/shard_map/dot_general | solution.py:107
  295.1 14.0 %convolution_convert_fusion.1 = bf16[1152,2152]{0,1:T(8,128)(2,1)} fusion(bf16[736,2152]{1,0:T(8,128)(2,1)S(1)} %copy-done.83, bf16[736,2152]{1,0:T(8,128)(2,1)S(1)} %copy-done.80, bf16[368,1152]{1,0:T(8,128)(2,1)} %collective-permute-done.9, bf16[368,1152]{1,0:T(8,128)(2,1)} %get-tuple-element.86, bf16[368,1152]{1,0:T(8,128)(2,1)} %collective-permute-done.8, ...), kind=kOutput, calls=%fused_computation.18 | convolution fusion | flops 7327198208 | bytes 14685184 | tf_op jit(solution)/shard_map/dot_general | solution.py:107
  348.0 19.6 %collective-permute-done.14 = bf16[368,1152]{1,0:T(8,128)(2,1)S(1)} collective-permute-done((bf16[368,1152]{1,0:T(8,128)(2,1)S(1)}, bf16[368,1152]{1,0:T(8,128)(2,1)S(1)}, u32[]{:S(2)}, u32[]{:S(2)}) %collective-permute-start.14) | collective-permute-done | bytes 847904 | tf_op jit(solution)/shard_map/ppermute | solution.py:116
  369.0 11.6 %multiply_reduce_fusion = (f32[8,736]{1,0:T(8,128)S(1)}, f32[8,736,736]{1,2,0:T(8,128)}) fusion(f32[8,736,736]{1,2,0:T(8,128)} %get-tuple-element.112, f32[8,736]{1,0:T(8,128)S(1)} %log_add_fusion, bf16[736,8,72]{0,2,1:T(8,128)(2,1)S(1)} %bitcast.236, bf16[736,8,72]{0,2,1:T(8,128)(2,1)S(1)} %bitcast.235), kind=kOutput, calls=%fused_computation.1 | convolution fusion | flops 637028608 | bytes 36411392 | tf_op jit(solution)/shard_map/qhe,khe->hqk/dot_general | solution.py:80
  380.6 12.7 %multiply_convert_fusion = bf16[8,736,736]{1,2,0:T(8,128)(2,1)S(1)} fusion(f32[8,736,736]{1,2,0:T(8,128)} %get-tuple-element.117, f32[8,736,736]{1,2,0:T(8,128)} %get-tuple-element.112, f32[8,736]{1,0:T(8,128)S(1)} %get-tuple-element.116, f32[8,736]{1,0:T(8,128)S(1)} %log_add_fusion), kind=kLoop, calls=%fused_computation | loop fusion | flops 17334272 | bytes 43382784 | tf_op jit(solution)/shard_map/convert_element_type | solution.py:84
  399.6 9.9 %fusion.161 = bf16[8,72,736]{2,1,0:T(8,128)(2,1)} fusion(bf16[736,8,72]{0,2,1:T(8,128)(2,1)S(1)} %bitcast.237, f32[8,736,736]{1,2,0:T(8,128)} %get-tuple-element.112, f32[8,736]{1,0:T(8,128)S(1)} %log_add_fusion), kind=kOutput, calls=%fused_computation.213 | convolution fusion | flops 633124864 | bytes 19053568 | tf_op jit(solution)/shard_map/hqk,qhe->khe/dot_general | solution.py:85
  410.9 9.9 %fusion.158 = bf16[8,72,736]{2,1,0:T(8,128)(2,1)} fusion(bf16[736,8,72]{0,2,1:T(8,128)(2,1)S(1)} %bitcast.238, f32[8,736,736]{1,2,0:T(8,128)} %get-tuple-element.110, f32[8,736]{1,0:T(8,128)S(1)} %log_add_fusion.1), kind=kOutput, calls=%fused_computation.212 | convolution fusion | flops 633124864 | bytes 19053568 | tf_op jit(solution)/shard_map/hqk,qhe->khe/dot_general | solution.py:85
  420.9 12.0 %multiply_reduce_fusion.1 = (f32[8,736]{1,0:T(8,128)S(1)}, f32[8,736,736]{1,2,0:T(8,128)}) fusion(f32[8,736,736]{1,2,0:T(8,128)} %get-tuple-element.110, f32[8,736]{1,0:T(8,128)S(1)} %log_add_fusion.1, bf16[736,8,72]{0,2,1:T(8,128)(2,1)S(1)} %bitcast.239, bf16[736,8,72]{0,2,1:T(8,128)(2,1)S(1)} %bitcast.233), kind=kOutput, calls=%fused_computation.4 | convolution fusion | flops 637028608 | bytes 36411392 | tf_op jit(solution)/shard_map/qhe,khe->hqk/dot_general | solution.py:80
  439.2 13.1 %multiply_convert_fusion.1 = bf16[8,736,736]{1,2,0:T(8,128)(2,1)S(1)} fusion(f32[8,736,736]{1,2,0:T(8,128)} %get-tuple-element.115, f32[8,736,736]{1,2,0:T(8,128)} %get-tuple-element.110, f32[8,736]{1,0:T(8,128)S(1)} %get-tuple-element.114, f32[8,736]{1,0:T(8,128)S(1)} %log_add_fusion.1), kind=kLoop, calls=%fused_computation.3 | loop fusion | flops 17334272 | bytes 43382784 | tf_op jit(solution)/shard_map/convert_element_type | solution.py:84
  458.5 10.3 %convolution_convert_fusion.2 = bf16[1152,1728]{0,1:T(8,128)(2,1)} fusion(bf16[368,1152]{1,0:T(8,128)(2,1)S(1)} %copy-done.77, bf16[368,1152]{1,0:T(8,128)(2,1)S(1)} %copy-done.49, bf16[368,1152]{1,0:T(8,128)(2,1)S(1)} %copy-done.79, bf16[368,1152]{1,0:T(8,128)(2,1)} %get-tuple-element.77, bf16[736,576]{0,1:T(8,128)(2,1)S(1)} %bitcast.225, ...), kind=kOutput, calls=%fused_computation.30 | convolution fusion | flops 5906571264 | bytes 12460032 | tf_op jit(solution)/shard_map/dot_general | solution.py:107
  493.8 11.8 %collective-permute-done.7 = bf16[368,1152]{1,0:T(8,128)(2,1)} collective-permute-done((bf16[368,1152]{1,0:T(8,128)(2,1)}, bf16[368,1152]{1,0:T(8,128)(2,1)}, u32[]{:S(2)}, u32[]{:S(2)}) %collective-permute-start.7) | collective-permute-done | bytes 847904 | tf_op jit(solution)/shard_map/ppermute | solution.py:116
  533.4 23.4 %convert_reduce_fusion.1 = f32[1728]{0:T(1024)S(1)} fusion(bf16[736,576]{0,1:T(8,128)(2,1)S(1)} %bitcast.227, bf16[736,576]{0,1:T(8,128)(2,1)S(1)} %bitcast.217, bf16[736,576]{0,1:T(8,128)(2,1)S(1)} %bitcast.207, bf16[736,576]{0,1:T(8,128)(2,1)S(1)} %bitcast.230, bf16[736,576]{0,1:T(8,128)(2,1)S(1)} %bitcast.220, bf16[736,576]{0,1:T(8,128)(2,1)S(1)} %bitcast.210), kind=kLoop, calls=%fused_computation.19 | loop fusion | flops 33065280 | bytes 5094144 | tf_op jit(solution)/shard_map/reduce_sum | solution.py:233
  564.0 39.7 %psum.7 = f32[13520]{0:T(1024)S(1)} all-reduce(f32[13520]{0:T(1024)S(1)} %constant_dynamic-update-slice_fusion), channel_id=1, replica_groups=mesh['fsdp'=16,'tp'=2] {'fsdp','tp'}, use_global_device_ids=true, to_apply=%region_39.40 | all-reduce | flops 13520 | bytes 108160 | tf_op jit(solution)/shard_map/psum | solution.py:254
  614.4 38.4 %reduce-scatter.17.cloned.1.call-done = bf16[1,72,2152]{2,1,0:T(8,128)(2,1)} async-done(((bf16[16,72,2152]{2,1,0:T(8,128)(2,1)}), bf16[1,72,2152]{2,1,0:T(8,128)(2,1)}) %reduce-scatter.17.cloned.1.call-update) | async-done | bytes 309904
  654.6 79.5 %reduce-scatter.15.cloned.1.call-done = bf16[1,72,2152]{2,1,0:T(8,128)(2,1)} async-done(((bf16[16,72,2152]{2,1,0:T(8,128)(2,1)}), bf16[1,72,2152]{2,1,0:T(8,128)(2,1)}) %reduce-scatter.15.cloned.1.call-update) | async-done | bytes 309904
  (342 shorter events, 258.9 us)
Async XLA Ops:
  7.2 56.7 %all-gather.5.cloned.1.call-start = ((), (), s32[]{:S(2)}) async-start(), calls=%async_computation.4 | async-start | bytes 4386816 | tf_op jit(solution)/shard_map/all_gather | solution.py:136
  9.4 111.3 %all-gather.7.cloned.1.call-start = ((), (), s32[]{:S(2)}) async-start(), calls=%async_computation.5 | async-start | bytes 1566720 | tf_op jit(solution)/shard_map/all_gather | solution.py:136
  10.2 191.6 %all-gather.9.cloned.1.call-start = ((), (), s32[]{:S(2)}) async-start(), calls=%async_computation.6 | async-start | bytes 5326848 | tf_op jit(solution)/shard_map/all_gather | solution.py:136
  10.9 227.2 %all-gather.11.cloned.1.call-start = ((), (), s32[]{:S(2)}) async-start(), calls=%async_computation.7 | async-start | bytes 5326848 | tf_op jit(solution)/shard_map/all_gather | solution.py:136
  16.4 22.7 %collective-permute-start.4 = (bf16[368,1152]{1,0:T(8,128)(2,1)S(1)}, bf16[368,1152]{1,0:T(8,128)(2,1)S(1)}, u32[]{:S(2)}, u32[]{:S(2)}) collective-permute-start(bf16[368,1152]{1,0:T(8,128)(2,1)S(1)} %get-tuple-element.78), channel_id=1, source_target_pairs={{0,1},{1,0},{2,3},{3,2},{4,5},{5,4},{6,7},{7,6},{8,9},{9,8},{10,11... | collective-permute-start | bytes 2543624 | tf_op jit(solution)/shard_map/ppermute | solution.py:116
  19.4 58.4 %collective-permute-start = (bf16[368,1152]{1,0:T(8,128)(2,1)}, bf16[368,1152]{1,0:T(8,128)(2,1)S(1)}, u32[]{:S(2)}, u32[]{:S(2)}) collective-permute-start(bf16[368,1152]{1,0:T(8,128)(2,1)} %get-tuple-element.77), channel_id=1, source_target_pairs={{0,1},{1,0},{2,3},{3,2},{4,5},{5,4},{6,7},{7,6},{8,9},{9,8},{10,11... | collective-permute-start | bytes 2543624 | tf_op jit(solution)/shard_map/ppermute | solution.py:116
  19.4 591.3 %reduce-scatter.13.cloned.1.call-start = ((), (), s32[]{:S(2)}) async-start(), calls=%async_computation.9 | async-start | bytes 1566720
  124.0 30.8 %collective-permute-start.1 = (bf16[368,1152]{1,0:T(8,128)(2,1)}, bf16[368,1152]{1,0:T(8,128)(2,1)}, u32[]{:S(2)}, u32[]{:S(2)}) collective-permute-start(bf16[368,1152]{1,0:T(8,128)(2,1)} %convolution_convert_fusion.10), channel_id=1, source_target_pairs={{0,1},{1,0},{2,3},{3,2},{4,5},{5,4},{6,7},{7,6},{8,9},{9,8},{10,11... | collective-permute-start | bytes 2543624 | tf_op jit(solution)/shard_map/ppermute | solution.py:116
  153.6 20.9 %collective-permute-start.5 = (bf16[368,1152]{1,0:T(8,128)(2,1)S(1)}, bf16[368,1152]{1,0:T(8,128)(2,1)S(1)}, u32[]{:S(2)}, u32[]{:S(2)}) collective-permute-start(bf16[368,1152]{1,0:T(8,128)(2,1)S(1)} %convolution_convert_fusion.8), channel_id=1, source_target_pairs={{0,1},{1,0},{2,3},{3,2},{4,5},{5,4},{6,7},{7,6},{8,9},{9,8},{10,11... | collective-permute-start | bytes 2543624 | tf_op jit(solution)/shard_map/ppermute | solution.py:116
  179.6 22.1 %collective-permute-start.6 = (bf16[368,1152]{1,0:T(8,128)(2,1)}, bf16[368,1152]{1,0:T(8,128)(2,1)}, u32[]{:S(2)}, u32[]{:S(2)}) collective-permute-start(bf16[368,1152]{1,0:T(8,128)(2,1)} %get-tuple-element.102), channel_id=1, source_target_pairs={{0,1},{1,0},{2,3},{3,2},{4,5},{5,4},{6,7},{7,6},{8,9},{9,8},{10,11... | collective-permute-start | bytes 2543624 | tf_op jit(solution)/shard_map/ppermute | solution.py:116
  181.3 86.4 %collective-permute-start.8 = (bf16[368,1152]{1,0:T(8,128)(2,1)}, bf16[368,1152]{1,0:T(8,128)(2,1)}, u32[]{:S(2)}, u32[]{:S(2)}) collective-permute-start(bf16[368,1152]{1,0:T(8,128)(2,1)} %get-tuple-element.85), channel_id=1, source_target_pairs={{0,1},{1,0},{2,3},{3,2},{4,5},{5,4},{6,7},{7,6},{8,9},{9,8},{10,11... | collective-permute-start | bytes 2543624 | tf_op jit(solution)/shard_map/ppermute | solution.py:116
  183.0 55.0 %collective-permute-start.9 = (bf16[368,1152]{1,0:T(8,128)(2,1)}, bf16[368,1152]{1,0:T(8,128)(2,1)}, u32[]{:S(2)}, u32[]{:S(2)}) collective-permute-start(bf16[368,1152]{1,0:T(8,128)(2,1)} %get-tuple-element.86), channel_id=1, source_target_pairs={{0,1},{1,0},{2,3},{3,2},{4,5},{5,4},{6,7},{7,6},{8,9},{9,8},{10,11... | collective-permute-start | bytes 2543624 | tf_op jit(solution)/shard_map/ppermute | solution.py:116
  183.4 72.8 %collective-permute-start.2 = (bf16[368,1152]{1,0:T(8,128)(2,1)}, bf16[368,1152]{1,0:T(8,128)(2,1)}, u32[]{:S(2)}, u32[]{:S(2)}) collective-permute-start(bf16[368,1152]{1,0:T(8,128)(2,1)} %get-tuple-element.101), channel_id=1, source_target_pairs={{0,1},{1,0},{2,3},{3,2},{4,5},{5,4},{6,7},{7,6},{8,9},{9,8},{10,11... | collective-permute-start | bytes 2543624 | tf_op jit(solution)/shard_map/ppermute | solution.py:116
  252.6 73.7 %collective-permute-start.11 = (bf16[368,1152]{1,0:T(8,128)(2,1)}, bf16[368,1152]{1,0:T(8,128)(2,1)}, u32[]{:S(2)}, u32[]{:S(2)}) collective-permute-start(bf16[368,1152]{1,0:T(8,128)(2,1)} %convolution_convert_fusion.5), channel_id=1, source_target_pairs={{0,1},{1,0},{2,3},{3,2},{4,5},{5,4},{6,7},{7,6},{8,9},{9,8},{10,11... | collective-permute-start | bytes 2543624 | tf_op jit(solution)/shard_map/ppermute | solution.py:116
  280.5 52.6 %collective-permute-start.10 = (bf16[368,1152]{1,0:T(8,128)(2,1)}, bf16[368,1152]{1,0:T(8,128)(2,1)}, u32[]{:S(2)}, u32[]{:S(2)}) collective-permute-start(bf16[368,1152]{1,0:T(8,128)(2,1)} %convolution_convert_fusion.6), channel_id=1, source_target_pairs={{0,1},{1,0},{2,3},{3,2},{4,5},{5,4},{6,7},{7,6},{8,9},{9,8},{10,11... | collective-permute-start | bytes 2543624 | tf_op jit(solution)/shard_map/ppermute | solution.py:116
  345.7 21.9 %collective-permute-start.14 = (bf16[368,1152]{1,0:T(8,128)(2,1)S(1)}, bf16[368,1152]{1,0:T(8,128)(2,1)S(1)}, u32[]{:S(2)}, u32[]{:S(2)}) collective-permute-start(bf16[368,1152]{1,0:T(8,128)(2,1)S(1)} %convert_element_type.297), channel_id=1, source_target_pairs={{0,1},{1,0},{2,3},{3,2},{4,5},{5,4},{6,7},{7,6},{8,9},{9,8},{10,11... | collective-permute-start | bytes 2543624 | tf_op jit(solution)/shard_map/ppermute | solution.py:116
  347.4 62.1 %collective-permute-start.12 = (bf16[368,1152]{1,0:T(8,128)(2,1)S(1)}, bf16[368,1152]{1,0:T(8,128)(2,1)S(1)}, u32[]{:S(2)}, u32[]{:S(2)}) collective-permute-start(bf16[368,1152]{1,0:T(8,128)(2,1)S(1)} %convert_element_type.281), channel_id=1, source_target_pairs={{0,1},{1,0},{2,3},{3,2},{4,5},{5,4},{6,7},{7,6},{8,9},{9,8},{10,11... | collective-permute-start | bytes 2543624 | tf_op jit(solution)/shard_map/ppermute | solution.py:116
  439.2 173.1 %reduce-scatter.11.cloned.1.call-start = ((), (), s32[]{:S(2)}) async-start(), calls=%async_computation.8 | async-start | bytes 4386816 | tf_op jit(solution)/shard_map/reduce_scatter | solution.py:140
  475.3 177.5 %reduce-scatter.17.cloned.1.call-start = ((), (), s32[]{:S(2)}) async-start(), calls=%async_computation.11 | async-start | bytes 5326848
  476.0 258.2 %reduce-scatter.15.cloned.1.call-start = ((), (), s32[]{:S(2)}) async-start(), calls=%async_computation.10 | async-start | bytes 5326848
  484.4 21.3 %collective-permute-start.7 = (bf16[368,1152]{1,0:T(8,128)(2,1)}, bf16[368,1152]{1,0:T(8,128)(2,1)}, u32[]{:S(2)}, u32[]{:S(2)}) collective-permute-start(bf16[368,1152]{1,0:T(8,128)(2,1)} %convolution_convert_fusion.7), channel_id=1, source_target_pairs={{0,1},{1,0},{2,3},{3,2},{4,5},{5,4},{6,7},{7,6},{8,9},{9,8},{10,11... | collective-permute-start | bytes 2543624 | tf_op jit(solution)/shard_map/ppermute | solution.py:116
  492.0 22.8 %collective-permute-start.3 = (bf16[368,1152]{1,0:T(8,128)(2,1)}, bf16[368,1152]{1,0:T(8,128)(2,1)}, u32[]{:S(2)}, u32[]{:S(2)}) collective-permute-start(bf16[368,1152]{1,0:T(8,128)(2,1)} %convolution_convert_fusion.9), channel_id=1, source_target_pairs={{0,1},{1,0},{2,3},{3,2},{4,5},{5,4},{6,7},{7,6},{8,9},{9,8},{10,11... | collective-permute-start | bytes 2543624 | tf_op jit(solution)/shard_map/ppermute | solution.py:116
  528.7 28.6 %collective-permute-start.15 = (bf16[368,1152]{1,0:T(8,128)(2,1)S(1)}, bf16[368,1152]{1,0:T(8,128)(2,1)S(1)}, u32[]{:S(2)}, u32[]{:S(2)}) collective-permute-start(bf16[368,1152]{1,0:T(8,128)(2,1)S(1)} %convolution_convert_fusion.3), channel_id=1, source_target_pairs={{0,1},{1,0},{2,3},{3,2},{4,5},{5,4},{6,7},{7,6},{8,9},{9,8},{10,11... | collective-permute-start | bytes 2543624 | tf_op jit(solution)/shard_map/ppermute | solution.py:116
  533.1 26.3 %collective-permute-start.13 = (bf16[368,1152]{1,0:T(8,128)(2,1)S(1)}, bf16[368,1152]{1,0:T(8,128)(2,1)S(1)}, u32[]{:S(2)}, u32[]{:S(2)}) collective-permute-start(bf16[368,1152]{1,0:T(8,128)(2,1)S(1)} %convolution_convert_fusion.4), channel_id=1, source_target_pairs={{0,1},{1,0},{2,3},{3,2},{4,5},{5,4},{6,7},{7,6},{8,9},{9,8},{10,11... | collective-permute-start | bytes 2543624 | tf_op jit(solution)/shard_map/ppermute | solution.py:116
  (86 other events, 1030.3 us)
Sparse Core Ops, SparseCore 0:
  10.9 52.9 all-gather.4
  66.1 37.8 all-gather.6
  106.1 53.7 all-gather.8
  161.8 53.4 all-gather.10
  439.3 57.4 reduce-scatter.12
  500.6 70.9 reduce-scatter.10
  575.6 77.1 reduce-scatter.16
  657.4 76.7 reduce-scatter.14
